TPU v7x, 32 devices: a whole 2x2x4 slice. The times are simulated.
32 devices in a mesh: row: 4 (over y, core), col: 8 (over z, x).
Axes of the slice: x: 2, y: 2, z: 4, core: 2. Of those that a mesh axis runs over, the one named last changes fastest.
Arguments:
- child_vectors: bfloat16 [2, 2048, 16384], P(None, 'row', 'col'), may hold values from -6 to 6
- merge_position: int32 [2, 16384], P(None, 'col'), may hold values from 0 to 32767, as said below
- pole_frac: float32 [2, 16384], P(None, 'col'), may hold values from 0 to 0.3
- weights: float32 [2, 16384], P(None, 'col'), may hold values from -3 to 3, as said below
- retained: int32 [2, 16384], P(None, 'col'), may hold values from 0 to 1, as said below
- root_index: int32 [512], replicated, may hold values from 0 to 32766
- root_offset: float32 [512], replicated, may hold values from 0.55 to 0.75
Outputs:
- merged: bfloat16 [2, 2048, 512], P(None, ('row', 'col'))
Inputs may be any that keep to these rules, and one draw needn't show every extreme that they name: `merge_position`: each merged position 0 to 32767 occurs exactly once over both children. The first pole of each aligned block of 2048 poles of a child is retained; elsewhere whole aligned blocks of 512 poles may be deflated. `weights`: magnitudes lie between 0.3 and 3.
All inputs are finite; a program needn't handle non-finite values.
Results may differ from a plain program's by a relative error of at most 0.015.
Values may be sent and summed in bfloat16 or wider, within the bound.
No kernel may reach another device: no remote copies, remote signals or barrier semaphores. Data moves between devices by JAX's collectives and lax.ppermute only.
A program may use at most 64 MiB of HBM per device.

v0:
```python
import jax
import jax.numpy as jnp
from jax import lax
from jax.sharding import PartitionSpec as P

PANEL = 128


def local(child_vectors, merge_position, pole_frac, weights, retained, root_index, root_offset):
    position, fraction, weight, keep_mask = (merge_position, pole_frac, weights, retained)
    scaled = keep_mask.astype(jnp.float32) * weight
    panel_count = root_index.shape[0] // PANEL
    results = []
    for number in range(panel_count):
        first_col = number * PANEL
        root_rows = root_index[first_col : first_col + PANEL]
        root_parts = root_offset[first_col : first_col + PANEL]
        spacing = (position[:, :, None] - root_rows[None, None, :]).astype(jnp.float32) + (
            fraction[:, :, None] - root_parts[None, None, :]
        )
        raw_panel = scaled[:, :, None] / spacing
        squares = jnp.sum(raw_panel * raw_panel, axis=(0, 1))
        panel_block = (raw_panel * lax.rsqrt(lax.psum(squares, "col"))[None, None, :]).astype(
            jnp.bfloat16
        )
        partial_value = jnp.einsum(
            "crh,chm->crm", child_vectors, panel_block, preferred_element_type=jnp.float32
        )
        results.append(
            lax.psum_scatter(
                partial_value.astype(jnp.bfloat16), "col", scatter_dimension=1, tiled=True
            )
        )
    return jnp.concatenate(results, axis=2)


def solution(mesh):
    return jax.shard_map(
        local,
        mesh=mesh,
        in_specs=(
            P(None, "row", "col"),
            P(None, "col"),
            P(None, "col"),
            P(None, "col"),
            P(None, "col"),
            P(),
            P(),
        ),
        out_specs=P(None, ("row", "col"), None),
        check_vma=False,
    )
```

profile of v0, /device:TPU:0, one launch (start us, length us, event | category | flops | bytes accessed | tf_op | source)
XLA Modules:
  0.0 139.6 jit_solution(11144587394085508906)
XLA Ops:
  6.5 0.0 all-reduce.8.cloned.1.call-start
  6.5 0.8 fusion.28
  7.4 0.8 fusion.29
  8.2 0.7 convert_multiply_fusion
  9.0 3.1 %multiply_reduce_fusion.3 = (f32[128]{0:T(128)S(1)}, f32[128]{0:T(128)S(1)}, f32[128]{0:T(128)S(1)}, f32[128]{0:T(128)S(1)}) fusion(f32[128]{0:T(128)S(1)} %get-tuple-element.23, f32[2,2048]{1,0:T(2,128)} %param.9, s32[128]{0:T(128)S(1)} %get-tuple-element.19, s32[2,2048]{1,0:T(2,128)} %param.8, f32[2,2048]{1,0:T(2,128)S(1)} %convert_multiply_fusion, ...), kind=kLoop, calls=%fused_computation.10 | loop fusion | flops 14679552 | bytes 55296 | tf_op jit(solution)/shard_map/reduce_sum | solution.py:22
  12.1 23.1 %all-reduce.4 = (f32[128]{0:T(128)S(1)}, f32[128]{0:T(128)S(1)}, f32[128]{0:T(128)S(1)}, f32[128]{0:T(128)S(1)}) all-reduce(f32[128]{0:T(128)S(1)} %get-tuple-element.8, f32[128]{0:T(128)S(1)} %get-tuple-element.7, f32[128]{0:T(128)S(1)} %get-tuple-element.6, f32[128]{0:T(128)S(1)} %get-tuple-element.5), channel_id=1, replica_groups=mesh['row'=4,'col'=8] {'col'}, use_global_device_ids=true, to_apply=%region_10.0 | all-reduce | flops 512 | bytes 4096 | tf_op jit(solution)/shard_map/psum | solution.py:23
  35.2 0.0 copy-start
  35.2 0.0 copy-start.1
  35.2 3.8 %fusion.1 = bf16[2,512,128]{1,2,0:T(8,128)(2,1)S(1)} fusion(bf16[2,512,2048]{2,1,0:T(8,128)(2,1)} %param.7, f32[128]{0:T(128)S(1)} %rsqrt.13, f32[128]{0:T(128)S(1)} %get-tuple-element.22, s32[128]{0:T(128)S(1)} %get-tuple-element.18, f32[2,2048]{1,0:T(2,128)} %param.9, s32[2,2048]{1,0:T(2,128)} %param.8, f32[2,2048]{1,0:T(2,128)S(1)} %convert_multiply_fusion), kind=kOutput, calls=%fused_computation.17 | convolution fusion | flops 540672000 | bytes 4507136 | tf_op jit(solution)/shard_map/crh,chm->crm/dot_general | solution.py:26
  39.0 0.9 copy.10
  39.9 0.0 copy-done
  39.9 0.0 copy-done.1
  39.9 3.7 %fusion.2 = bf16[2,512,128]{1,2,0:T(8,128)(2,1)S(1)} fusion(bf16[2,512,2048]{2,1,0:T(8,128)(2,1)} %param.7, f32[128]{0:T(128)S(1)} %rsqrt.14, f32[128]{0:T(128)S(1)} %get-tuple-element.24, s32[128]{0:T(128)S(1)} %get-tuple-element.20, f32[2,2048]{1,0:T(2,128)S(1)} %copy-done, s32[2,2048]{1,0:T(2,128)S(1)} %copy-done.1, f32[2,2048]{1,0:T(2,128)S(1)} %convert_multiply_fusion), kind=kOutput, calls=%fused_computation.18 | convolution fusion | flops 540672000 | bytes 4507136 | tf_op jit(solution)/shard_map/crh,chm->crm/dot_general | solution.py:26
  43.6 0.9 copy.11
  44.5 3.7 %fusion = bf16[2,512,128]{1,2,0:T(8,128)(2,1)S(1)} fusion(bf16[2,512,2048]{2,1,0:T(8,128)(2,1)} %param.7, f32[128]{0:T(128)S(1)} %rsqrt.12, f32[128]{0:T(128)S(1)} %get-tuple-element.23, f32[2,2048]{1,0:T(2,128)S(1)} %copy-done, s32[128]{0:T(128)S(1)} %get-tuple-element.19, s32[2,2048]{1,0:T(2,128)S(1)} %copy-done.1, f32[2,2048]{1,0:T(2,128)S(1)} %convert_multiply_fusion), kind=kOutput, calls=%fused_computation.16 | convolution fusion | flops 540672000 | bytes 4507136 | tf_op jit(solution)/shard_map/crh,chm->crm/dot_general | solution.py:26
  48.3 0.9 copy.9
  49.1 0.0 copy-start.2
  49.1 3.7 %fusion.3 = bf16[2,512,128]{1,2,0:T(8,128)(2,1)S(1)} fusion(bf16[2,512,2048]{2,1,0:T(8,128)(2,1)} %param.7, f32[128]{0:T(128)S(1)} %rsqrt.15, f32[128]{0:T(128)S(1)} %get-tuple-element.21, s32[128]{0:T(128)S(1)} %get-tuple-element.17, f32[2,2048]{1,0:T(2,128)S(1)} %copy-done, s32[2,2048]{1,0:T(2,128)S(1)} %copy-done.1, f32[2,2048]{1,0:T(2,128)S(1)} %convert_multiply_fusion), kind=kOutput, calls=%fused_computation.19 | convolution fusion | flops 540672000 | bytes 4507136 | tf_op jit(solution)/shard_map/crh,chm->crm/dot_general | solution.py:26
  52.9 0.9 copy.12
  53.8 0.0 all-reduce.8.cloned.1.call-update
  53.8 0.0 copy-done.2
  53.8 0.6 dynamic-slice
  55.1 75.2 %all-reduce.8.cloned.1.call-done = (bf16[2,512,128]{2,0,1:T(2,128)(2,1)}, bf16[2,512,128]{2,0,1:T(2,128)(2,1)}, bf16[2,512,128]{2,0,1:T(2,128)(2,1)}, bf16[2,512,128]{2,0,1:T(2,128)(2,1)}) async-done(((bf16[2,512,128]{2,0,1:T(2,128)(2,1)}, bf16[2,512,128]{2,0,1:T(2,128)(2,1)}, bf16[2,512,128]{2,0,1:T(2,128)(2,1)}, bf16[2,512,128]{2,0,1:T(2,128)(2,1)}), (bf16[2,512,128]{2,0,1:T(2,128)(2,1)}, ...) | async-done | bytes 1048592
  130.3 0.8 constant_dynamic-slice_fusion.2
  131.1 0.8 constant_dynamic-slice_fusion
  131.9 0.2 pad_maximum_fusion
  132.1 0.7 copy.13
  (4 shorter events, 0.0 us)
Async XLA Ops:
  6.5 123.7 %all-reduce.8.cloned.1.call-start = ((), (), s32[]{:S(2)}) async-start(), calls=%async_computation | async-start | bytes 2097152
  35.2 4.7 %copy-start = (f32[2,2048]{1,0:T(2,128)S(1)}, f32[2,2048]{1,0:T(2,128)}, u32[]{:S(2)}) copy-start(f32[2,2048]{1,0:T(2,128)} %param.9) | copy-start | bytes 49156
  35.2 4.7 %copy-start.1 = (s32[2,2048]{1,0:T(2,128)S(1)}, s32[2,2048]{1,0:T(2,128)}, u32[]{:S(2)}) copy-start(s32[2,2048]{1,0:T(2,128)} %param.8) | copy-start | bytes 49156
  49.1 4.7 %copy-start.2 = (u32[32]{0:T(128)S(1)}, u32[32]{0:T(128)}, u32[]{:S(2)}) copy-start(u32[32]{0:T(128)} %constant.4) | copy-start | bytes 388
Sparse Core Ops, SparseCore 0:
  53.9 76.2 all-reduce.7
where the time goes:
time: 140 us
  waiting for transfers between devices  75.2 us (54%)
  blocking collectives  23.1 us (16%)
  matrix products  15 us (11%)
  between operations  14.1 us (10%)
  local copies, waits for them, and re-layouts  8.12 us (6%)
  other arithmetic  4.03 us (3%)
    unnamed x2, waiting for transfers between devices  75.2 us
    psum x1, blocking collectives, local(): lax.psum(squares, 'col')  23.1 us
    dot_general x4, matrix products, local(): jnp.einsum('crh,chm->crm', child_vectors, panel_block, preferred_element_...  15 us
    convert_element_type x4, local copies, waits for them, and re-layouts, local(): partial_value.astype(jnp.bfloat16)  3.53 us
    reduce_sum x1, other arithmetic, local(): squares = jnp.sum(raw_panel * raw_panel, axis=(0, 1))  3.14 us
  transfers between devices with their start and end apart: 1, of which 1 were waited for; matrix products, arithmetic and copies ran while one was open for 0% of the time, Pallas kernels for 0%

commit v1 on v0

v1 whole, which is shorter than its diff:
```python
import functools

import jax
import jax.numpy as jnp
from jax import lax
from jax.experimental import pallas as pl
from jax.experimental.pallas import tpu as pltpu
from jax.sharding import PartitionSpec as P

LANES = 128
VMEM = pl.BlockSpec(memory_space=pltpu.VMEM)
F32, BF16 = jnp.float32, jnp.bfloat16


def radices(n):
    near = min(4, n)
    return near, n // near


def child_kernel(child, near, far, *refs):
    pos_ref, frac_ref, weight_ref, kept_ref, root_ref, off_ref, vec_ref = refs[:7]
    outs = refs[7 : 7 + near]
    total_ref = refs[7 + near]
    vec, panel, poles, roots, sums, sems = refs[8 + near :]
    rows, depth = vec.shape
    cols = panel.shape[0]
    block = rows // (near * far)
    me = lax.rem(lax.axis_index("col"), near)

    copies = []
    for k in range(near):
        target = jnp.bitwise_xor(me, k)
        for h in range(far):
            first = pl.multiple_of((h * near + target) * block, block)
            copy = pltpu.make_async_copy(
                vec_ref.at[child, pl.ds(first, block), :],
                vec.at[pl.ds((k * far + h) * block, block), :],
                sems.at[k, h],
            )
            copy.start()
            copies.append(copy)

    own = pl.ds(child, 1)
    for number, row in enumerate(
        (
            pos_ref[own, :].astype(F32),
            frac_ref[own, :],
            kept_ref[own, :].astype(F32) * weight_ref[own, :],
        )
    ):
        poles[number] = jnp.broadcast_to(row, (8, depth))
    for first in range(0, cols, LANES):
        for number, ref in enumerate((root_ref, off_ref)):
            row = ref[:, first : first + LANES].astype(F32)
            roots[number, first : first + LANES, :] = jnp.broadcast_to(row, (LANES, LANES)).T

    def columns(step, carry):
        at = pl.ds(pl.multiple_of(step * 16, 16), 16)
        root = roots[0, at, :].reshape(2, 8, LANES)
        off = roots[1, at, :].reshape(2, 8, LANES)
        total = jnp.zeros((2, 8, LANES), F32)
        for first in range(0, depth, LANES):
            here = slice(first, first + LANES)
            spacing = (poles[0, :, here] - root) + (poles[1, :, here] - off)
            inverse = pl.reciprocal(spacing, approx=True)
            inverse = inverse * (2.0 - spacing * inverse)
            raw = poles[2, :, here] * inverse
            total = total + raw * raw
            panel[at, here] = raw.reshape(16, LANES).astype(BF16)
        sums[at, :] = total.reshape(16, LANES)
        return carry

    lax.fori_loop(0, cols // 16, columns, 0)
    for first in range(0, cols, LANES):
        here = slice(first, first + LANES)
        total_ref[:, here] = jnp.sum(sums[here, :].T, axis=0, keepdims=True)
    for copy in copies:
        copy.wait()
    width = min(256, cols)
    for first in range(0, cols, width):
        here = slice(first, first + width)
        part = lax.dot_general(
            vec[...], panel[here, :], (((1,), (1,)), ((), ())), preferred_element_type=F32
        ).astype(BF16)
        for k in range(near):
            outs[k][:, here] = part[k * far * block : (k + 1) * far * block]


def child_call(child, near, far, poles, roots, vectors):
    rows, depth = vectors.shape[1:]
    cols = roots[0].shape[1]
    return pl.pallas_call(
        functools.partial(child_kernel, child, near, far),
        out_shape=[jax.ShapeDtypeStruct((rows // near, cols), BF16)] * near
        + [jax.ShapeDtypeStruct((1, cols), F32)],
        in_specs=[VMEM] * 6 + [pl.BlockSpec(memory_space=pl.ANY)],
        out_specs=[VMEM] * (near + 1),
        scratch_shapes=[
            pltpu.VMEM((rows, depth), BF16),
            pltpu.VMEM((cols, depth), BF16),
            pltpu.VMEM((3, 8, depth), F32),
            pltpu.VMEM((2, cols, LANES), F32),
            pltpu.VMEM((cols, LANES), F32),
            pltpu.SemaphoreType.DMA((near, far)),
        ],
        compiler_params=pltpu.CompilerParams(vmem_limit_bytes=24 * 2**20),
        cost_estimate=pl.CostEstimate(
            flops=2 * rows * depth * cols, bytes_accessed=2 * rows * depth, transcendentals=depth * cols
        ),
    )(*poles, *roots, vectors)


def middle_kernel(near, far, *refs):
    parts, totals, (own_ref, *outs), total_ref = (
        refs[:near],
        refs[near : 2 * near],
        refs[2 * near : 2 * near + far],
        refs[2 * near + far],
    )
    block = own_ref.shape[0]
    me = lax.div(lax.axis_index("col"), near)
    for k in range(far):
        at = pl.ds(pl.multiple_of(jnp.bitwise_xor(me, k) * block, block), block)
        value = parts[0][at, :].astype(F32)
        for part in parts[1:]:
            value = value + part[at, :].astype(F32)
        if k:
            outs[k - 1][...] = value.astype(BF16)
        else:
            own_ref[...] = value
    total = totals[0][...]
    for part in totals[1:]:
        total = total + part[...]
    total_ref[...] = total


def middle_call(near, far, parts, totals):
    rows, cols = parts[0].shape
    shape = (rows // far, cols)
    return pl.pallas_call(
        functools.partial(middle_kernel, near, far),
        out_shape=[jax.ShapeDtypeStruct(shape, F32)]
        + [jax.ShapeDtypeStruct(shape, BF16)] * (far - 1)
        + [jax.ShapeDtypeStruct((1, cols), F32)],
        in_specs=[VMEM] * (2 * near),
        out_specs=[VMEM] * (far + 1),
    )(*parts, *totals)


def last_kernel(children, far, *refs):
    out_ref = refs[-1]
    per = 2 * far
    total = None
    for child in range(children):
        for ref in refs[child * per + far : (child + 1) * per]:
            total = ref[...] if total is None else total + ref[...]
    scale = lax.rsqrt(total)
    for child in range(children):
        value = refs[child * per][...]
        for ref in refs[child * per + 1 : child * per + far]:
            value = value + ref[...].astype(F32)
        out_ref[child] = (value * scale).astype(BF16)


def exchange(parts, stride, n):
    return [parts[0]] + [
        lax.ppermute(part, "col", [(i, i ^ (k * stride)) for i in range(n)])
        for k, part in enumerate(parts)
        if k
    ]


def solution(mesh):
    n = mesh.shape["col"]
    near, far = radices(n)

    def local(vectors, position, fraction, weight, retained, root_index, root_offset):
        children = vectors.shape[0]
        roots = (root_index[None, :], root_offset[None, :])
        ends = []
        for child in range(children):
            *parts, total = child_call(
                child, near, far, (position, fraction, weight, retained), roots, vectors
            )
            parts = exchange(parts, 1, n)
            totals = exchange([total] * near, 1, n)
            *parts, total = middle_call(near, far, parts, totals)
            parts = exchange(parts, near, n)
            totals = exchange([total] * far, near, n)
            ends += parts + totals
        block, cols = ends[0].shape
        return pl.pallas_call(
            functools.partial(last_kernel, children, far),
            out_shape=jax.ShapeDtypeStruct((children, block, cols), BF16),
            in_specs=[VMEM] * len(ends),
            out_specs=VMEM,
        )(*ends)

    return jax.shard_map(
        local,
        mesh=mesh,
        in_specs=(P(None, "row", "col"),) + (P(None, "col"),) * 4 + (P(), P()),
        out_specs=P(None, ("row", "col"), None),
        check_vma=False,
    )
```

time: 140 us -> 51.1 us (0.36)
  waiting for transfers between devices: 75.2 us -> 6.59 us
  blocking collectives: 23.1 us -> 0 us
  starting transfers between devices: 0.01 us -> 21.8 us
  matrix products: 15 us -> 0 us
  between operations: 14.1 us -> 0.2 us
  Pallas kernels: 0 us -> 12.9 us
  other arithmetic: 4.03 us -> 0 us
    unnamed x2 -> x0, waiting for transfers between devices: 75.2 us -> none
    psum x1 -> x0, blocking collectives: 23.1 us -> none  [local(): lax.psum(squares, 'col')]
    ppermute x0 -> x16, starting transfers between devices: none -> 21.8 us  [exchange(): lax.ppermute(part, 'col', [(i, i ^ k * stride) for i in range(n)])]
    dot_general x4 -> x0, matrix products: 15 us -> none  [local(): jnp.einsum('crh,chm->crm', child_vectors, panel_block, preferred_element_...]
    pallas_call x0 -> x5, Pallas kernels: none -> 12.9 us  [the longest x2 7.44 us: child_call(): pl.pallas_call(functools.partial(child_kernel, child, near, far), out_sha...]
    unnamed x9 -> x54, local copies, waits for them, and re-layouts: 2.24 us -> 9.06 us
    ppermute x0 -> x16, waiting for transfers between devices: none -> 6.59 us  [exchange(): lax.ppermute(part, 'col', [(i, i ^ k * stride) for i in range(n)])]
    convert_element_type x4 -> x0, local copies, waits for them, and re-layouts: 3.53 us -> none  [local(): partial_value.astype(jnp.bfloat16)]
  transfers between devices with their start and end apart: 1 -> 16, of which waited for: 1 -> 5; matrix products, arithmetic and copies ran while one was open for 0% -> 0% of each run, Pallas kernels for 0% -> 15%
where the time goes in v1:
time: 51.1 us; the launch traced here: 50.5 us
  starting transfers between devices  21.8 us (43%)
  Pallas kernels  12.9 us (25%)
  local copies, waits for them, and re-layouts  9.06 us (18%)
  waiting for transfers between devices  6.59 us (13%)
    ppermute x16, starting transfers between devices, exchange(): lax.ppermute(part, 'col', [(i, i ^ k * stride) for i in range(n)])  21.8 us
    unnamed x54, local copies, waits for them, and re-layouts  9.06 us
    pallas_call x2, Pallas kernels, child_call(): pl.pallas_call(functools.partial(child_kernel, child, near, far), out_sha...  7.44 us
    ppermute x16, waiting for transfers between devices, exchange(): lax.ppermute(part, 'col', [(i, i ^ k * stride) for i in range(n)])  6.59 us
    pallas_call x2, Pallas kernels, middle_call(): pl.pallas_call(functools.partial(middle_kernel, near, far), out_shape=[ja...  3.68 us
    pallas_call x1, Pallas kernels, local(): pl.pallas_call(functools.partial(last_kernel, children, far), out_shape=j...  1.74 us
  transfers between devices with their start and end apart: 16, of which 5 were waited for; matrix products, arithmetic and copies ran while one was open for 0% of the time, Pallas kernels for 15%

profile of v1, /device:TPU:0, one launch (start us, length us, event | category | flops | bytes accessed | tf_op | source)
XLA Modules:
  0.0 50.5 jit_solution(18350594921206213894)
XLA Ops:
  0.0 2.2 %copy-done = bf16[2,512,2048]{2,1,0:T(8,128)(2,1)S(1)} copy-done((bf16[2,512,2048]{2,1,0:T(8,128)(2,1)S(1)}, bf16[2,512,2048]{2,1,0:T(8,128)(2,1)}, u32[]{:S(2)}) %copy-start) | copy-done | bytes 4194328
  2.2 0.7 %copy-done.3 = s32[2,2048]{1,0:T(2,128)S(1)} copy-done((s32[2,2048]{1,0:T(2,128)S(1)}, s32[2,2048]{1,0:T(2,128)}, u32[]{:S(2)}) %copy-start.3) | copy-done | bytes 16408
  2.9 0.7 %copy-done.4 = f32[2,2048]{1,0:T(2,128)S(1)} copy-done((f32[2,2048]{1,0:T(2,128)S(1)}, f32[2,2048]{1,0:T(2,128)}, u32[]{:S(2)}) %copy-start.4) | copy-done | bytes 16408
  3.6 0.7 %copy-done.5 = f32[2,2048]{1,0:T(2,128)S(1)} copy-done((f32[2,2048]{1,0:T(2,128)S(1)}, f32[2,2048]{1,0:T(2,128)}, u32[]{:S(2)}) %copy-start.5) | copy-done | bytes 16408
  4.3 0.7 %copy-done.6 = s32[2,2048]{1,0:T(2,128)S(1)} copy-done((s32[2,2048]{1,0:T(2,128)S(1)}, s32[2,2048]{1,0:T(2,128)}, u32[]{:S(2)}) %copy-start.6) | copy-done | bytes 16408
  5.1 0.7 %copy-done.7 = s32[512]{0:T(512)S(1)} copy-done((s32[512]{0:T(512)S(1)}, s32[512]{0:T(512)}, u32[]{:S(2)}) %copy-start.7) | copy-done | bytes 2072
  5.7 0.7 %copy-done.8 = f32[512]{0:T(512)S(1)} copy-done((f32[512]{0:T(512)S(1)}, f32[512]{0:T(512)}, u32[]{:S(2)}) %copy-start.8) | copy-done | bytes 2072
  6.4 3.7 %shard_map.75 = (bf16[128,512]{1,0:T(8,128)(2,1)S(1)}, bf16[128,512]{1,0:T(8,128)(2,1)S(1)}, bf16[128,512]{1,0:T(8,128)(2,1)S(1)}, bf16[128,512]{1,0:T(8,128)(2,1)S(1)}, f32[1,512]{1,0:T(1,128)S(1)}) custom-call(s32[2,2048]{1,0:T(2,128)S(1)} %copy-done.3, f32[2,2048]{1,0:T(2,128)S(1)} %copy-done.4, f32[2,2048]{1,0:T(2,128)S(1)} %copy-done.5, ...), custom_call_target="tpu_custom_call" | custom-call | flops 1073741824 | bytes 2097152 | tf_op jit(solution)/shard_map/pallas_call | solution.py:92
  10.2 0.0 copy-start.2
  10.2 0.6 %copy-done.2 = bf16[128,512]{1,0:T(8,128)(2,1)} copy-done((bf16[128,512]{1,0:T(8,128)(2,1)}, bf16[128,512]{1,0:T(8,128)(2,1)S(1)}, u32[]{:S(2)}) %copy-start.2) | copy-done | bytes 131096
  10.8 2.9 %collective-permute-start.8 = (bf16[128,512]{1,0:T(8,128)(2,1)S(1)}, bf16[128,512]{1,0:T(8,128)(2,1)S(1)}, u32[]{:S(2)}, u32[]{:S(2)}) collective-permute-start(bf16[128,512]{1,0:T(8,128)(2,1)S(1)} %get-tuple-element.30), channel_id=1, source_target_pairs={{0,1},{1,0},{2,3},{3,2},{4,5},{5,4},{6,7},{7,6},{8,9},{9,8},{10,11... | collective-permute-start | bytes 393224 | tf_op jit(solution)/shard_map/ppermute | solution.py:167
  13.7 1.6 %collective-permute-start.13 = (f32[1,512]{1,0:T(1,128)S(1)}, f32[1,512]{1,0:T(1,128)S(1)}, u32[]{:S(2)}, u32[]{:S(2)}) collective-permute-start(f32[1,512]{1,0:T(1,128)S(1)} %get-tuple-element.33.refs_4_), channel_id=1, source_target_pairs={{0,3},{1,2},{2,1},{3,0},{4,7},{5,6},{6,5},{7,4},{8,11},{9,10},{10,... | collective-permute-start | bytes 6152 | tf_op jit(solution)/shard_map/ppermute | solution.py:167
  15.3 0.0 collective-permute-start.12
  15.3 1.9 %collective-permute-start.11 = (f32[1,512]{1,0:T(1,128)S(1)}, f32[1,512]{1,0:T(1,128)S(1)}, u32[]{:S(2)}, u32[]{:S(2)}) collective-permute-start(f32[1,512]{1,0:T(1,128)S(1)} %get-tuple-element.33.refs_4_), channel_id=1, source_target_pairs={{0,1},{1,0},{2,3},{3,2},{4,5},{5,4},{6,7},{7,6},{8,9},{9,8},{10,11... | collective-permute-start | bytes 6152 | tf_op jit(solution)/shard_map/ppermute | solution.py:167
  17.2 1.6 %collective-permute-start.9 = (bf16[128,512]{1,0:T(8,128)(2,1)S(1)}, bf16[128,512]{1,0:T(8,128)(2,1)S(1)}, u32[]{:S(2)}, u32[]{:S(2)}) collective-permute-start(bf16[128,512]{1,0:T(8,128)(2,1)S(1)} %get-tuple-element.31), channel_id=1, source_target_pairs={{0,2},{1,3},{2,0},{3,1},{4,6},{5,7},{6,4},{7,5},{8,10},{9,11},{10,... | collective-permute-start | bytes 393224 | tf_op jit(solution)/shard_map/ppermute | solution.py:167
  18.8 3.7 %shard_map.73 = (bf16[128,512]{1,0:T(8,128)(2,1)S(1)}, bf16[128,512]{1,0:T(8,128)(2,1)S(1)}, bf16[128,512]{1,0:T(8,128)(2,1)S(1)}, bf16[128,512]{1,0:T(8,128)(2,1)S(1)}, f32[1,512]{1,0:T(1,128)S(1)}) custom-call(s32[2,2048]{1,0:T(2,128)S(1)} %copy-done.3, f32[2,2048]{1,0:T(2,128)S(1)} %copy-done.4, f32[2,2048]{1,0:T(2,128)S(1)} %copy-done.5, ...), custom_call_target="tpu_custom_call" | custom-call | flops 1073741824 | bytes 2097152 | tf_op jit(solution)/shard_map/pallas_call | solution.py:92
  22.5 0.0 copy-start.1
  22.6 0.6 %copy-done.1 = bf16[128,512]{1,0:T(8,128)(2,1)} copy-done((bf16[128,512]{1,0:T(8,128)(2,1)}, bf16[128,512]{1,0:T(8,128)(2,1)S(1)}, u32[]{:S(2)}) %copy-start.1) | copy-done | bytes 131096
  23.2 0.0 collective-permute-done.13.refs_7_
  23.2 0.0 collective-permute-start.5
  23.2 0.0 collective-permute-done.12.refs_6_
  23.2 0.0 copy-start.21
  23.2 2.9 %collective-permute-start.10 = (bf16[128,512]{1,0:T(8,128)(2,1)S(1)}, bf16[128,512]{1,0:T(8,128)(2,1)S(1)}, u32[]{:S(2)}, u32[]{:S(2)}) collective-permute-start(bf16[128,512]{1,0:T(8,128)(2,1)S(1)} %get-tuple-element.32), channel_id=1, source_target_pairs={{0,3},{1,2},{2,1},{3,0},{4,7},{5,6},{6,5},{7,4},{8,11},{9,10},{10,... | collective-permute-start | bytes 393224 | tf_op jit(solution)/shard_map/ppermute | solution.py:167
  26.1 0.0 collective-permute-done.11.refs_5_
  26.1 0.5 %collective-permute-start = (bf16[128,512]{1,0:T(8,128)(2,1)S(1)}, bf16[128,512]{1,0:T(8,128)(2,1)S(1)}, u32[]{:S(2)}, u32[]{:S(2)}) collective-permute-start(bf16[128,512]{1,0:T(8,128)(2,1)S(1)} %get-tuple-element.22), channel_id=1, source_target_pairs={{0,1},{1,0},{2,3},{3,2},{4,5},{5,4},{6,7},{7,6},{8,9},{9,8},{10,11... | collective-permute-start | bytes 393224 | tf_op jit(solution)/shard_map/ppermute | solution.py:167
  26.7 1.1 %collective-permute-done.5.refs_7_ = f32[1,512]{1,0:T(1,128)S(1)} collective-permute-done((f32[1,512]{1,0:T(1,128)S(1)}, f32[1,512]{1,0:T(1,128)S(1)}, u32[]{:S(2)}, u32[]{:S(2)}) %collective-permute-start.5) | collective-permute-done | bytes 2080 | tf_op jit(solution)/shard_map/ppermute | solution.py:167
  27.8 0.5 collective-permute-start.1
  28.3 0.0 collective-permute-done.8.refs_1_
  28.3 1.5 %collective-permute-start.2 = (bf16[128,512]{1,0:T(8,128)(2,1)S(1)}, bf16[128,512]{1,0:T(8,128)(2,1)S(1)}, u32[]{:S(2)}, u32[]{:S(2)}) collective-permute-start(bf16[128,512]{1,0:T(8,128)(2,1)S(1)} %get-tuple-element.24), channel_id=1, source_target_pairs={{0,3},{1,2},{2,1},{3,0},{4,7},{5,6},{6,5},{7,4},{8,11},{9,10},{10,... | collective-permute-start | bytes 393224 | tf_op jit(solution)/shard_map/ppermute | solution.py:167
  29.8 0.0 collective-permute-done.9.refs_2_
  29.8 0.3 collective-permute-start.4
  30.1 0.4 collective-permute-done.10.refs_3_
  30.5 1.8 %collective-permute-start.3 = (f32[1,512]{1,0:T(1,128)S(1)}, f32[1,512]{1,0:T(1,128)S(1)}, u32[]{:S(2)}, u32[]{:S(2)}) collective-permute-start(f32[1,512]{1,0:T(1,128)S(1)} %get-tuple-element.25.refs_4_), channel_id=1, source_target_pairs={{0,1},{1,0},{2,3},{3,2},{4,5},{5,4},{6,7},{7,6},{8,9},{9,8},{10,11... | collective-permute-start | bytes 6152 | tf_op jit(solution)/shard_map/ppermute | solution.py:167
  32.4 0.0 copy-done.10
  32.4 0.0 copy-done.20
  32.4 0.0 copy-done.22
  32.4 0.0 copy-done.11
  32.4 0.0 copy-done.13
  32.4 0.0 copy-done.16
  32.4 1.8 %shard_map.76 = (f32[64,512]{1,0:T(8,128)}, bf16[64,512]{1,0:T(8,128)(2,1)}, f32[1,512]{1,0:T(1,128)}) custom-call(bf16[128,512]{1,0:T(8,128)(2,1)} %copy-done.2, bf16[128,512]{1,0:T(8,128)(2,1)} %copy-done.11, bf16[128,512]{1,0:T(8,128)(2,1)} %copy-done.13, bf16[128,512]{1,0:T(8,128)(2,1)} %copy-done.16, f32[1,512]{1,0:T(1,128)} %copy-done.10, ...), custom_call_target="tpu_custom_call" | custom-call | tf_op jit(solution)/shard_map/pallas_call | solution.py:140
  34.3 0.4 collective-permute-done.4.refs_6_
  34.6 3.3 %collective-permute-start.14 = (bf16[64,512]{1,0:T(8,128)(2,1)}, bf16[64,512]{1,0:T(8,128)(2,1)S(1)}, u32[]{:S(2)}, u32[]{:S(2)}) collective-permute-start(bf16[64,512]{1,0:T(8,128)(2,1)} %get-tuple-element.35), channel_id=1, source_target_pairs={{0,4},{1,5},{2,6},{3,7},{4,0},{5,1},{6,2},{7,3},{8,12},{9,13},{10,... | collective-permute-start | bytes 196616 | tf_op jit(solution)/shard_map/ppermute | solution.py:167
  37.9 0.0 collective-permute-done.3.refs_5_
  37.9 0.0 collective-permute-done.refs_1_
  38.0 0.0 collective-permute-done.1.refs_2_
  38.0 0.0 collective-permute-done.2.refs_3_
  38.0 0.5 copy-done.24
  38.5 0.1 copy-done.12
  38.6 0.1 copy-done.14
  38.7 0.0 copy-done.15
  38.7 1.8 %shard_map.74 = (f32[64,512]{1,0:T(8,128)}, bf16[64,512]{1,0:T(8,128)(2,1)}, f32[1,512]{1,0:T(1,128)}) custom-call(bf16[128,512]{1,0:T(8,128)(2,1)} %copy-done.1, bf16[128,512]{1,0:T(8,128)(2,1)} %copy-done.12, bf16[128,512]{1,0:T(8,128)(2,1)} %copy-done.14, bf16[128,512]{1,0:T(8,128)(2,1)} %copy-done.15, f32[1,512]{1,0:T(1,128)} %copy-done.9, ...), custom_call_target="tpu_custom_call" | custom-call | tf_op jit(solution)/shard_map/pallas_call | solution.py:140
  40.5 0.0 collective-permute-start.6
  40.5 2.9 %collective-permute-start.15 = (f32[1,512]{1,0:T(1,128)}, f32[1,512]{1,0:T(1,128)S(1)}, u32[]{:S(2)}, u32[]{:S(2)}) collective-permute-start(f32[1,512]{1,0:T(1,128)} %get-tuple-element.36.refs_6_), channel_id=1, source_target_pairs={{0,4},{1,5},{2,6},{3,7},{4,0},{5,1},{6,2},{7,3},{8,12},{9,13},{10,... | collective-permute-start | bytes 6152 | tf_op jit(solution)/shard_map/ppermute | solution.py:167
  43.5 0.0 collective-permute-start.7
  43.5 3.1 %collective-permute-done.15.refs_7_ = f32[1,512]{1,0:T(1,128)S(1)} collective-permute-done((f32[1,512]{1,0:T(1,128)}, f32[1,512]{1,0:T(1,128)S(1)}, u32[]{:S(2)}, u32[]{:S(2)}) %collective-permute-start.15) | collective-permute-done | bytes 2080 | tf_op jit(solution)/shard_map/ppermute | solution.py:167
  46.7 1.5 %collective-permute-done.7.refs_3_ = f32[1,512]{1,0:T(1,128)S(1)} collective-permute-done((f32[1,512]{1,0:T(1,128)}, f32[1,512]{1,0:T(1,128)S(1)}, u32[]{:S(2)}, u32[]{:S(2)}) %collective-permute-start.7) | collective-permute-done | bytes 2080 | tf_op jit(solution)/shard_map/ppermute | solution.py:167
  48.2 0.0 collective-permute-done.14.refs_5_
  48.2 0.0 collective-permute-done.6.refs_1_
  48.2 0.0 copy-start.18
  48.2 0.0 copy-done.25
  48.2 0.5 %copy-done.26 = f32[1,512]{1,0:T(1,128)} copy-done((f32[1,512]{1,0:T(1,128)}, f32[1,512]{1,0:T(1,128)S(1)}, u32[]{:S(2)}) %copy-start.26) | copy-done | bytes 2072
  48.7 0.1 copy-done.17
  48.8 0.0 copy-done.18
  48.8 1.7 %shard_map.77 = bf16[2,64,512]{2,1,0:T(8,128)(2,1)} custom-call(f32[64,512]{1,0:T(8,128)} %get-tuple-element.26.refs_0_, bf16[64,512]{1,0:T(8,128)(2,1)} %copy-done.18, f32[1,512]{1,0:T(1,128)} %get-tuple-element.28.refs_2_, f32[1,512]{1,0:T(1,128)} %copy-done.26, f32[64,512]{1,0:T(8,128)} %get-tuple-element.34.refs_4_, bf16[64,512]{1,0:T(8,128)(2,1)} %copy-done.17, ...), custom_call_target="tpu_custom_call" | custom-call | tf_op jit(solution)/shard_map/pallas_call | solution.py:192
  (27 shorter events, 0.0 us)
Async XLA Ops:
  0.0 2.2 %copy-start = (bf16[2,512,2048]{2,1,0:T(8,128)(2,1)S(1)}, bf16[2,512,2048]{2,1,0:T(8,128)(2,1)}, u32[]{:S(2)}) copy-start(bf16[2,512,2048]{2,1,0:T(8,128)(2,1)} %refs_6_.3) | copy-start | bytes 12582916
  2.2 0.7 %copy-start.3 = (s32[2,2048]{1,0:T(2,128)S(1)}, s32[2,2048]{1,0:T(2,128)}, u32[]{:S(2)}) copy-start(s32[2,2048]{1,0:T(2,128)} %refs_0_.3) | copy-start | bytes 49156
  2.9 0.7 %copy-start.4 = (f32[2,2048]{1,0:T(2,128)S(1)}, f32[2,2048]{1,0:T(2,128)}, u32[]{:S(2)}) copy-start(f32[2,2048]{1,0:T(2,128)} %refs_1_.3) | copy-start | bytes 49156
  3.6 0.7 %copy-start.5 = (f32[2,2048]{1,0:T(2,128)S(1)}, f32[2,2048]{1,0:T(2,128)}, u32[]{:S(2)}) copy-start(f32[2,2048]{1,0:T(2,128)} %refs_2_.3) | copy-start | bytes 49156
  4.3 0.7 %copy-start.6 = (s32[2,2048]{1,0:T(2,128)S(1)}, s32[2,2048]{1,0:T(2,128)}, u32[]{:S(2)}) copy-start(s32[2,2048]{1,0:T(2,128)} %refs_3_.3) | copy-start | bytes 49156
  5.1 0.7 %copy-start.7 = (s32[512]{0:T(512)S(1)}, s32[512]{0:T(512)}, u32[]{:S(2)}) copy-start(s32[512]{0:T(512)} %param.12) | copy-start | bytes 6148
  5.7 0.7 %copy-start.8 = (f32[512]{0:T(512)S(1)}, f32[512]{0:T(512)}, u32[]{:S(2)}) copy-start(f32[512]{0:T(512)} %param.13) | copy-start | bytes 6148
  10.2 0.7 %copy-start.2 = (bf16[128,512]{1,0:T(8,128)(2,1)}, bf16[128,512]{1,0:T(8,128)(2,1)S(1)}, u32[]{:S(2)}) copy-start(bf16[128,512]{1,0:T(8,128)(2,1)S(1)} %get-tuple-element.29.refs_0_) | copy-start | bytes 393220
  10.8 21.6 %copy-start.10 = (f32[1,512]{1,0:T(1,128)}, f32[1,512]{1,0:T(1,128)S(1)}, u32[]{:S(2)}) copy-start(f32[1,512]{1,0:T(1,128)S(1)} %get-tuple-element.33.refs_4_) | copy-start | bytes 6148
  10.8 17.5 %collective-permute-start.8 = (bf16[128,512]{1,0:T(8,128)(2,1)S(1)}, bf16[128,512]{1,0:T(8,128)(2,1)S(1)}, u32[]{:S(2)}, u32[]{:S(2)}) collective-permute-start(bf16[128,512]{1,0:T(8,128)(2,1)S(1)} %get-tuple-element.30), channel_id=1, source_target_pairs={{0,1},{1,0},{2,3},{3,2},{4,5},{5,4},{6,7},{7,6},{8,9},{9,8},{10,11... | collective-permute-start | bytes 393224 | tf_op jit(solution)/shard_map/ppermute | solution.py:167
  13.7 9.5 %collective-permute-start.13 = (f32[1,512]{1,0:T(1,128)S(1)}, f32[1,512]{1,0:T(1,128)S(1)}, u32[]{:S(2)}, u32[]{:S(2)}) collective-permute-start(f32[1,512]{1,0:T(1,128)S(1)} %get-tuple-element.33.refs_4_), channel_id=1, source_target_pairs={{0,3},{1,2},{2,1},{3,0},{4,7},{5,6},{6,5},{7,4},{8,11},{9,10},{10,... | collective-permute-start | bytes 6152 | tf_op jit(solution)/shard_map/ppermute | solution.py:167
  15.3 7.9 %collective-permute-start.12 = (f32[1,512]{1,0:T(1,128)S(1)}, f32[1,512]{1,0:T(1,128)S(1)}, u32[]{:S(2)}, u32[]{:S(2)}) collective-permute-start(f32[1,512]{1,0:T(1,128)S(1)} %get-tuple-element.33.refs_4_), channel_id=1, source_target_pairs={{0,2},{1,3},{2,0},{3,1},{4,6},{5,7},{6,4},{7,5},{8,10},{9,11},{10,... | collective-permute-start | bytes 6152 | tf_op jit(solution)/shard_map/ppermute | solution.py:167
  15.3 10.8 %collective-permute-start.11 = (f32[1,512]{1,0:T(1,128)S(1)}, f32[1,512]{1,0:T(1,128)S(1)}, u32[]{:S(2)}, u32[]{:S(2)}) collective-permute-start(f32[1,512]{1,0:T(1,128)S(1)} %get-tuple-element.33.refs_4_), channel_id=1, source_target_pairs={{0,1},{1,0},{2,3},{3,2},{4,5},{5,4},{6,7},{7,6},{8,9},{9,8},{10,11... | collective-permute-start | bytes 6152 | tf_op jit(solution)/shard_map/ppermute | solution.py:167
  17.2 12.5 %collective-permute-start.9 = (bf16[128,512]{1,0:T(8,128)(2,1)S(1)}, bf16[128,512]{1,0:T(8,128)(2,1)S(1)}, u32[]{:S(2)}, u32[]{:S(2)}) collective-permute-start(bf16[128,512]{1,0:T(8,128)(2,1)S(1)} %get-tuple-element.31), channel_id=1, source_target_pairs={{0,2},{1,3},{2,0},{3,1},{4,6},{5,7},{6,4},{7,5},{8,10},{9,11},{10,... | collective-permute-start | bytes 393224 | tf_op jit(solution)/shard_map/ppermute | solution.py:167
  22.5 0.7 %copy-start.1 = (bf16[128,512]{1,0:T(8,128)(2,1)}, bf16[128,512]{1,0:T(8,128)(2,1)S(1)}, u32[]{:S(2)}) copy-start(bf16[128,512]{1,0:T(8,128)(2,1)S(1)} %get-tuple-element.21.refs_0_) | copy-start | bytes 393220
  23.2 14.8 %copy-start.9 = (f32[1,512]{1,0:T(1,128)}, f32[1,512]{1,0:T(1,128)S(1)}, u32[]{:S(2)}) copy-start(f32[1,512]{1,0:T(1,128)S(1)} %get-tuple-element.25.refs_4_) | copy-start | bytes 6148
  23.2 9.2 %copy-start.20 = (f32[1,512]{1,0:T(1,128)}, f32[1,512]{1,0:T(1,128)S(1)}, u32[]{:S(2)}) copy-start(f32[1,512]{1,0:T(1,128)S(1)} %collective-permute-done.13.refs_7_) | copy-start | bytes 6148
  23.2 4.6 %collective-permute-start.5 = (f32[1,512]{1,0:T(1,128)S(1)}, f32[1,512]{1,0:T(1,128)S(1)}, u32[]{:S(2)}, u32[]{:S(2)}) collective-permute-start(f32[1,512]{1,0:T(1,128)S(1)} %get-tuple-element.25.refs_4_), channel_id=1, source_target_pairs={{0,3},{1,2},{2,1},{3,0},{4,7},{5,6},{6,5},{7,4},{8,11},{9,10},{10,... | collective-permute-start | bytes 6152 | tf_op jit(solution)/shard_map/ppermute | solution.py:167
  23.2 9.2 %copy-start.21 = (f32[1,512]{1,0:T(1,128)}, f32[1,512]{1,0:T(1,128)S(1)}, u32[]{:S(2)}) copy-start(f32[1,512]{1,0:T(1,128)S(1)} %collective-permute-done.12.refs_6_) | copy-start | bytes 6148
  23.2 7.3 %collective-permute-start.10 = (bf16[128,512]{1,0:T(8,128)(2,1)S(1)}, bf16[128,512]{1,0:T(8,128)(2,1)S(1)}, u32[]{:S(2)}, u32[]{:S(2)}) collective-permute-start(bf16[128,512]{1,0:T(8,128)(2,1)S(1)} %get-tuple-element.32), channel_id=1, source_target_pairs={{0,3},{1,2},{2,1},{3,0},{4,7},{5,6},{6,5},{7,4},{8,11},{9,10},{10,... | collective-permute-start | bytes 393224 | tf_op jit(solution)/shard_map/ppermute | solution.py:167
  26.1 6.3 %copy-start.22 = (f32[1,512]{1,0:T(1,128)}, f32[1,512]{1,0:T(1,128)S(1)}, u32[]{:S(2)}) copy-start(f32[1,512]{1,0:T(1,128)S(1)} %collective-permute-done.11.refs_5_) | copy-start | bytes 6148
  26.1 11.8 %collective-permute-start = (bf16[128,512]{1,0:T(8,128)(2,1)S(1)}, bf16[128,512]{1,0:T(8,128)(2,1)S(1)}, u32[]{:S(2)}, u32[]{:S(2)}) collective-permute-start(bf16[128,512]{1,0:T(8,128)(2,1)S(1)} %get-tuple-element.22), channel_id=1, source_target_pairs={{0,1},{1,0},{2,3},{3,2},{4,5},{5,4},{6,7},{7,6},{8,9},{9,8},{10,11... | collective-permute-start | bytes 393224 | tf_op jit(solution)/shard_map/ppermute | solution.py:167
  27.8 10.2 %copy-start.19 = (f32[1,512]{1,0:T(1,128)}, f32[1,512]{1,0:T(1,128)S(1)}, u32[]{:S(2)}) copy-start(f32[1,512]{1,0:T(1,128)S(1)} %collective-permute-done.5.refs_7_) | copy-start | bytes 6148
  27.8 10.2 %collective-permute-start.1 = (bf16[128,512]{1,0:T(8,128)(2,1)S(1)}, bf16[128,512]{1,0:T(8,128)(2,1)S(1)}, u32[]{:S(2)}, u32[]{:S(2)}) collective-permute-start(bf16[128,512]{1,0:T(8,128)(2,1)S(1)} %get-tuple-element.23), channel_id=1, source_target_pairs={{0,2},{1,3},{2,0},{3,1},{4,6},{5,7},{6,4},{7,5},{8,10},{9,11},{10,... | collective-permute-start | bytes 393224 | tf_op jit(solution)/shard_map/ppermute | solution.py:167
  28.3 4.1 %copy-start.11 = (bf16[128,512]{1,0:T(8,128)(2,1)}, bf16[128,512]{1,0:T(8,128)(2,1)S(1)}, u32[]{:S(2)}) copy-start(bf16[128,512]{1,0:T(8,128)(2,1)S(1)} %collective-permute-done.8.refs_1_) | copy-start | bytes 393220
  28.3 9.7 %collective-permute-start.2 = (bf16[128,512]{1,0:T(8,128)(2,1)S(1)}, bf16[128,512]{1,0:T(8,128)(2,1)S(1)}, u32[]{:S(2)}, u32[]{:S(2)}) collective-permute-start(bf16[128,512]{1,0:T(8,128)(2,1)S(1)} %get-tuple-element.24), channel_id=1, source_target_pairs={{0,3},{1,2},{2,1},{3,0},{4,7},{5,6},{6,5},{7,4},{8,11},{9,10},{10,... | collective-permute-start | bytes 393224 | tf_op jit(solution)/shard_map/ppermute | solution.py:167
  29.8 2.6 %copy-start.13 = (bf16[128,512]{1,0:T(8,128)(2,1)}, bf16[128,512]{1,0:T(8,128)(2,1)S(1)}, u32[]{:S(2)}) copy-start(bf16[128,512]{1,0:T(8,128)(2,1)S(1)} %collective-permute-done.9.refs_2_) | copy-start | bytes 393220
  29.8 4.9 %collective-permute-start.4 = (f32[1,512]{1,0:T(1,128)S(1)}, f32[1,512]{1,0:T(1,128)S(1)}, u32[]{:S(2)}, u32[]{:S(2)}) collective-permute-start(f32[1,512]{1,0:T(1,128)S(1)} %get-tuple-element.25.refs_4_), channel_id=1, source_target_pairs={{0,2},{1,3},{2,0},{3,1},{4,6},{5,7},{6,4},{7,5},{8,10},{9,11},{10,... | collective-permute-start | bytes 6152 | tf_op jit(solution)/shard_map/ppermute | solution.py:167
  30.5 1.9 %copy-start.16 = (bf16[128,512]{1,0:T(8,128)(2,1)}, bf16[128,512]{1,0:T(8,128)(2,1)S(1)}, u32[]{:S(2)}) copy-start(bf16[128,512]{1,0:T(8,128)(2,1)S(1)} %collective-permute-done.10.refs_3_) | copy-start | bytes 393220
  30.5 7.4 %collective-permute-start.3 = (f32[1,512]{1,0:T(1,128)S(1)}, f32[1,512]{1,0:T(1,128)S(1)}, u32[]{:S(2)}, u32[]{:S(2)}) collective-permute-start(f32[1,512]{1,0:T(1,128)S(1)} %get-tuple-element.25.refs_4_), channel_id=1, source_target_pairs={{0,1},{1,0},{2,3},{3,2},{4,5},{5,4},{6,7},{7,6},{8,9},{9,8},{10,11... | collective-permute-start | bytes 6152 | tf_op jit(solution)/shard_map/ppermute | solution.py:167
  34.6 3.4 %copy-start.23 = (f32[1,512]{1,0:T(1,128)}, f32[1,512]{1,0:T(1,128)S(1)}, u32[]{:S(2)}) copy-start(f32[1,512]{1,0:T(1,128)S(1)} %collective-permute-done.4.refs_6_) | copy-start | bytes 6148
  34.6 13.5 %collective-permute-start.14 = (bf16[64,512]{1,0:T(8,128)(2,1)}, bf16[64,512]{1,0:T(8,128)(2,1)S(1)}, u32[]{:S(2)}, u32[]{:S(2)}) collective-permute-start(bf16[64,512]{1,0:T(8,128)(2,1)} %get-tuple-element.35), channel_id=1, source_target_pairs={{0,4},{1,5},{2,6},{3,7},{4,0},{5,1},{6,2},{7,3},{8,12},{9,13},{10,... | collective-permute-start | bytes 196616 | tf_op jit(solution)/shard_map/ppermute | solution.py:167
  37.9 0.6 %copy-start.24 = (f32[1,512]{1,0:T(1,128)}, f32[1,512]{1,0:T(1,128)S(1)}, u32[]{:S(2)}) copy-start(f32[1,512]{1,0:T(1,128)S(1)} %collective-permute-done.3.refs_5_) | copy-start | bytes 6148
  37.9 0.6 %copy-start.12 = (bf16[128,512]{1,0:T(8,128)(2,1)}, bf16[128,512]{1,0:T(8,128)(2,1)S(1)}, u32[]{:S(2)}) copy-start(bf16[128,512]{1,0:T(8,128)(2,1)S(1)} %collective-permute-done.refs_1_) | copy-start | bytes 393220
  38.0 0.7 %copy-start.14 = (bf16[128,512]{1,0:T(8,128)(2,1)}, bf16[128,512]{1,0:T(8,128)(2,1)S(1)}, u32[]{:S(2)}) copy-start(bf16[128,512]{1,0:T(8,128)(2,1)S(1)} %collective-permute-done.1.refs_2_) | copy-start | bytes 393220
  38.0 0.7 %copy-start.15 = (bf16[128,512]{1,0:T(8,128)(2,1)}, bf16[128,512]{1,0:T(8,128)(2,1)S(1)}, u32[]{:S(2)}) copy-start(bf16[128,512]{1,0:T(8,128)(2,1)S(1)} %collective-permute-done.2.refs_3_) | copy-start | bytes 393220
  40.5 7.6 %collective-permute-start.6 = (bf16[64,512]{1,0:T(8,128)(2,1)}, bf16[64,512]{1,0:T(8,128)(2,1)S(1)}, u32[]{:S(2)}, u32[]{:S(2)}) collective-permute-start(bf16[64,512]{1,0:T(8,128)(2,1)} %get-tuple-element.27), channel_id=1, source_target_pairs={{0,4},{1,5},{2,6},{3,7},{4,0},{5,1},{6,2},{7,3},{8,12},{9,13},{10,... | collective-permute-start | bytes 196616 | tf_op jit(solution)/shard_map/ppermute | solution.py:167
  40.5 6.1 %collective-permute-start.15 = (f32[1,512]{1,0:T(1,128)}, f32[1,512]{1,0:T(1,128)S(1)}, u32[]{:S(2)}, u32[]{:S(2)}) collective-permute-start(f32[1,512]{1,0:T(1,128)} %get-tuple-element.36.refs_6_), channel_id=1, source_target_pairs={{0,4},{1,5},{2,6},{3,7},{4,0},{5,1},{6,2},{7,3},{8,12},{9,13},{10,... | collective-permute-start | bytes 6152 | tf_op jit(solution)/shard_map/ppermute | solution.py:167
  43.5 4.7 %collective-permute-start.7 = (f32[1,512]{1,0:T(1,128)}, f32[1,512]{1,0:T(1,128)S(1)}, u32[]{:S(2)}, u32[]{:S(2)}) collective-permute-start(f32[1,512]{1,0:T(1,128)} %get-tuple-element.28.refs_2_), channel_id=1, source_target_pairs={{0,4},{1,5},{2,6},{3,7},{4,0},{5,1},{6,2},{7,3},{8,12},{9,13},{10,... | collective-permute-start | bytes 6152 | tf_op jit(solution)/shard_map/ppermute | solution.py:167
  46.7 1.5 %copy-start.25 = (f32[1,512]{1,0:T(1,128)}, f32[1,512]{1,0:T(1,128)S(1)}, u32[]{:S(2)}) copy-start(f32[1,512]{1,0:T(1,128)S(1)} %collective-permute-done.15.refs_7_) | copy-start | bytes 6148
  48.2 0.6 %copy-start.26 = (f32[1,512]{1,0:T(1,128)}, f32[1,512]{1,0:T(1,128)S(1)}, u32[]{:S(2)}) copy-start(f32[1,512]{1,0:T(1,128)S(1)} %collective-permute-done.7.refs_3_) | copy-start | bytes 6148
  48.2 0.6 %copy-start.17 = (bf16[64,512]{1,0:T(8,128)(2,1)}, bf16[64,512]{1,0:T(8,128)(2,1)S(1)}, u32[]{:S(2)}) copy-start(bf16[64,512]{1,0:T(8,128)(2,1)S(1)} %collective-permute-done.14.refs_5_) | copy-start | bytes 196612
  48.2 0.6 %copy-start.18 = (bf16[64,512]{1,0:T(8,128)(2,1)}, bf16[64,512]{1,0:T(8,128)(2,1)S(1)}, u32[]{:S(2)}) copy-start(bf16[64,512]{1,0:T(8,128)(2,1)S(1)} %collective-permute-done.6.refs_1_) | copy-start | bytes 196612

commit v2 on v0

v2 whole, which is shorter than its diff:
```python
import functools

import jax
import jax.numpy as jnp
from jax import lax
from jax.experimental import pallas as pl
from jax.experimental.pallas import tpu as pltpu
from jax.sharding import PartitionSpec as P

LANES = 128
VMEM = pl.BlockSpec(memory_space=pltpu.VMEM)
ANY = pl.BlockSpec(memory_space=pl.ANY)
F32, BF16 = jnp.float32, jnp.bfloat16
SMALL = pltpu.CompilerParams(vmem_limit_bytes=6 * 2**20)


def radices(n):
    near = min(4, n)
    return near, n // near


def tail_rows(tiles):
    return -(-3 * tiles // 16) * 16


def write_tail(total, ref, first):
    tiles = total.shape[0]
    high = total.astype(BF16).astype(F32)
    rest = total - high
    middle = rest.astype(BF16).astype(F32)
    pieces = [high, middle, rest - middle]
    spare = tail_rows(tiles) - 3 * tiles
    if spare:
        pieces.append(jnp.zeros((spare, LANES), F32))
    ref[first:, :] = jnp.concatenate(pieces, axis=0).astype(BF16)


def read_tail(ref, tiles):
    tail = ref[ref.shape[0] - tail_rows(tiles) :, :].astype(F32)
    return (tail[2 * tiles : 3 * tiles] + tail[tiles : 2 * tiles]) + tail[:tiles]


def child_kernel(child, near, far, *refs):
    pole_refs, root_refs, vec_ref = refs[:4], refs[4:6], refs[6]
    outs = refs[7 : 7 + near]
    vec, panels, poles, pole_in, kept_in, root_in, index_in, roots, sums, staged, sems, in_sems, out_sems = refs[7 + near :]
    rows, depth = vec.shape
    width = panels.shape[1]
    cols = roots.shape[1]
    tiles = cols // LANES
    part = rows // near
    block = part // far
    me = lax.rem(lax.axis_index("col"), near)

    pos_ref, frac_ref, weight_ref, kept_ref = pole_refs
    small = [
        pltpu.make_async_copy(source, target, in_sems.at[number])
        for number, (source, target) in enumerate(
            (
                (root_refs[0], index_in),
                (root_refs[1], root_in),
                (pos_ref, kept_in.at[0]),
                (frac_ref, pole_in.at[0]),
                (weight_ref, pole_in.at[1]),
                (kept_ref, kept_in.at[1]),
            )
        )
    ]
    for copy in small:
        copy.start()
    large = []
    for k in range(near):
        target = jnp.bitwise_xor(me, k)
        for h in range(far):
            first = pl.multiple_of((h * near + target) * block, block)
            large.append(
                pltpu.make_async_copy(
                    vec_ref.at[child, pl.ds(first, block), :],
                    vec.at[pl.ds(k * part + h * block, block), :],
                    sems.at[k, h],
                )
            )
    for copy in large:
        copy.start()
    for copy in small:
        copy.wait()

    for first in range(0, cols, LANES):
        for number, row in enumerate((index_in[:, first : first + LANES].astype(F32), root_in[:, first : first + LANES])):
            roots[number, first : first + LANES, :] = jnp.broadcast_to(row, (LANES, LANES)).T
    own = slice(child, child + 1)
    for number, row in enumerate(
        (
            kept_in[0, own, :].astype(F32),
            pole_in[0, own, :],
            kept_in[1, own, :].astype(F32) * pole_in[1, own, :],
        )
    ):
        poles[number] = jnp.broadcast_to(row, (8, depth))

    def form(first_col, panel):
        for row in range(0, width, 16):
            at = slice(first_col + row, first_col + row + 16)
            root = roots[0, at, :].reshape(2, 8, LANES)
            off = roots[1, at, :].reshape(2, 8, LANES)
            total = jnp.zeros((2, 8, LANES), F32)
            for first in range(0, depth, LANES):
                here = slice(first, first + LANES)
                spacing = (poles[0, :, here] - root) + (poles[1, :, here] - off)
                inverse = pl.reciprocal(spacing, approx=True)
                inverse = inverse * (2.0 - spacing * inverse)
                raw = poles[2, :, here] * inverse
                total = total + raw * raw
                panel[row : row + 16, here] = raw.reshape(16, LANES).astype(BF16)
            sums[at, :] = total.reshape(16, LANES)

    def send(first_col, panel):
        value = lax.dot_general(
            vec[...], panel[...], (((1,), (1,)), ((), ())), preferred_element_type=F32
        ).astype(BF16)
        for k in range(near):
            for first in range(0, width, LANES):
                tile = (first_col + first) // LANES
                staged[k, tile * part : (tile + 1) * part, :] = value[
                    k * part : (k + 1) * part, first : first + LANES
                ]

    firsts = list(range(0, cols, width))
    form(firsts[0], panels.at[0])
    for copy in large:
        copy.wait()
    for number, first in enumerate(firsts):
        if number + 1 < len(firsts):
            form(firsts[number + 1], panels.at[(number + 1) % 2])
        else:
            total = jnp.concatenate(
                [
                    jnp.sum(sums[at : at + LANES, :].T, axis=0, keepdims=True)
                    for at in range(0, cols, LANES)
                ],
                axis=0,
            )
            for k in range(near):
                write_tail(total, staged.at[k], tiles * part)
        send(first, panels.at[number % 2])
    copies = [pltpu.make_async_copy(staged.at[k], outs[k], out_sems.at[k]) for k in range(near)]
    for copy in copies:
        copy.start()
    for copy in copies:
        copy.wait()


def child_call(child, near, far, poles, roots, vectors):
    children, rows, depth = vectors.shape
    cols = roots[0].shape[1]
    tiles = cols // LANES
    width = min(256, cols)
    shape = (tiles * (rows // near) + tail_rows(tiles), LANES)
    return pl.pallas_call(
        functools.partial(child_kernel, child, near, far),
        out_shape=[jax.ShapeDtypeStruct(shape, BF16)] * near,
        in_specs=[ANY] * 7,
        out_specs=[ANY] * near,
        scratch_shapes=[
            pltpu.VMEM((rows, depth), BF16),
            pltpu.VMEM((2, width, depth), BF16),
            pltpu.VMEM((3, 8, depth), F32),
            pltpu.VMEM((2, children, depth), F32),
            pltpu.VMEM((2, children, depth), jnp.int32),
            pltpu.VMEM((1, cols), F32),
            pltpu.VMEM((1, cols), jnp.int32),
            pltpu.VMEM((2, cols, LANES), F32),
            pltpu.VMEM((cols, LANES), F32),
            pltpu.VMEM((near, *shape), BF16),
            pltpu.SemaphoreType.DMA((near, far)),
            pltpu.SemaphoreType.DMA((6,)),
            pltpu.SemaphoreType.DMA((near,)),
        ],
        compiler_params=pltpu.CompilerParams(vmem_limit_bytes=60 * 2**20),
        cost_estimate=pl.CostEstimate(
            flops=2 * rows * depth * cols, bytes_accessed=2 * rows * depth, transcendentals=depth * cols
        ),
    )(*poles, *roots, vectors)


def middle_kernel(far, tiles, *refs):
    parts, (own_ref, total_ref, *outs) = refs[: -1 - far], refs[-1 - far :]
    block = own_ref.shape[0] // tiles
    me = lax.div(lax.axis_index("col"), len(parts))
    total = read_tail(parts[0], tiles)
    for part in parts[1:]:
        total = total + read_tail(part, tiles)
    total_ref[...] = total
    for out in outs:
        write_tail(total, out, tiles * block)
    for k in range(far):
        target = jnp.bitwise_xor(me, k)
        for tile in range(tiles):
            at = pl.ds(pl.multiple_of((tile * far + target) * block, block), block)
            value = parts[0][at, :].astype(F32)
            for part in parts[1:]:
                value = value + part[at, :].astype(F32)
            here = slice(tile * block, (tile + 1) * block)
            if k:
                outs[k - 1][here, :] = value.astype(BF16)
            else:
                own_ref[here, :] = value


def middle_call(far, tiles, parts):
    rows = (parts[0].shape[0] - tail_rows(tiles)) // far
    return pl.pallas_call(
        functools.partial(middle_kernel, far, tiles),
        out_shape=[
            jax.ShapeDtypeStruct((rows, LANES), F32),
            jax.ShapeDtypeStruct((tiles, LANES), F32),
        ]
        + [jax.ShapeDtypeStruct((rows + tail_rows(tiles), LANES), BF16)] * (far - 1),
        in_specs=[VMEM] * len(parts),
        out_specs=[VMEM] * (far + 1),
        compiler_params=SMALL,
    )(*parts)


def last_kernel(children, far, *refs):
    out_ref = refs[-1]
    tiles = out_ref.shape[2] // LANES
    block = out_ref.shape[1]
    groups = [refs[child * (far + 1) : (child + 1) * (far + 1)] for child in range(children)]
    total = None
    for _, own_total, *parts in groups:
        for value in [own_total[...]] + [read_tail(part, tiles) for part in parts]:
            total = value if total is None else total + value
    scale = lax.rsqrt(total)
    for child, (own, _, *parts) in enumerate(groups):
        for tile in range(tiles):
            here = slice(tile * block, (tile + 1) * block)
            value = own[here, :]
            for part in parts:
                value = value + part[here, :].astype(F32)
            out_ref[child, :, tile * LANES : (tile + 1) * LANES] = (
                value * scale[tile : tile + 1, :]
            ).astype(BF16)


def exchange(parts, stride, n):
    return [parts[0]] + [
        lax.ppermute(part, "col", [(i, i ^ (k * stride)) for i in range(n)])
        for k, part in enumerate(parts)
        if k
    ]


def solution(mesh):
    n = mesh.shape["col"]
    near, far = radices(n)

    def local(vectors, position, fraction, weight, retained, root_index, root_offset):
        children, rows, _ = vectors.shape
        cols = root_index.shape[0]
        tiles = cols // LANES
        roots = (root_index[None, :], root_offset[None, :])
        poles = (position, fraction, weight, retained)
        ends = []
        for child in range(children):
            parts = exchange(child_call(child, near, far, poles, roots, vectors), 1, n)
            own, total, *parts = middle_call(far, tiles, parts)
            ends += [own, total] + exchange([own] + parts, near, n)[1:]
        return pl.pallas_call(
            functools.partial(last_kernel, children, far),
            out_shape=jax.ShapeDtypeStruct((children, rows // n, cols), BF16),
            in_specs=[VMEM] * len(ends),
            out_specs=VMEM,
            compiler_params=SMALL,
        )(*ends)

    return jax.shard_map(
        local,
        mesh=mesh,
        in_specs=(P(None, "row", "col"),) + (P(None, "col"),) * 4 + (P(), P()),
        out_specs=P(None, ("row", "col"), None),
        check_vma=False,
    )
```

time: 140 us -> 32.7 us (0.23)
  waiting for transfers between devices: 75.2 us -> 8.01 us
  blocking collectives: 23.1 us -> 0 us
  matrix products: 15 us -> 0 us
  between operations: 14.1 us -> 0.06 us
  starting transfers between devices: 0.01 us -> 13.5 us
  Pallas kernels: 0 us -> 10 us
  local copies, waits for them, and re-layouts: 8.12 us -> 0.91 us
  other arithmetic: 4.03 us -> 0 us
    unnamed x2 -> x0, waiting for transfers between devices: 75.2 us -> none
    psum x1 -> x0, blocking collectives: 23.1 us -> none  [local(): lax.psum(squares, 'col')]
    dot_general x4 -> x0, matrix products: 15 us -> none  [local(): jnp.einsum('crh,chm->crm', child_vectors, panel_block, preferred_element_...]
    ppermute x0 -> x8, starting transfers between devices: none -> 13.5 us  [exchange(): lax.ppermute(part, 'col', [(i, i ^ k * stride) for i in range(n)])]
    pallas_call x0 -> x5, Pallas kernels: none -> 10 us  [the longest x2 9.15 us: child_call(): pl.pallas_call(functools.partial(child_kernel, child, near, far), out_sha...]
    ppermute x0 -> x8, waiting for transfers between devices: none -> 8.01 us  [exchange(): lax.ppermute(part, 'col', [(i, i ^ k * stride) for i in range(n)])]
    convert_element_type x4 -> x0, local copies, waits for them, and re-layouts: 3.53 us -> none  [local(): partial_value.astype(jnp.bfloat16)]
    reduce_sum x1 -> x0, other arithmetic: 3.14 us -> none  [local(): squares = jnp.sum(raw_panel * raw_panel, axis=(0, 1))]
  transfers between devices with their start and end apart: 1 -> 8, of which waited for: 1 -> 3; matrix products, arithmetic and copies ran while one was open for 0% -> 0% of each run, Pallas kernels for 0% -> 15%
where the time goes in v2:
time: 32.7 us; the launch traced here: 32.5 us
  starting transfers between devices  13.5 us (41%)
  Pallas kernels  10 us (31%)
  waiting for transfers between devices  8.01 us (24%)
  local copies, waits for them, and re-layouts  0.91 us (3%)
    ppermute x8, starting transfers between devices, exchange(): lax.ppermute(part, 'col', [(i, i ^ k * stride) for i in range(n)])  13.5 us
    pallas_call x2, Pallas kernels, child_call(): pl.pallas_call(functools.partial(child_kernel, child, near, far), out_sha...  9.15 us
    ppermute x8, waiting for transfers between devices, exchange(): lax.ppermute(part, 'col', [(i, i ^ k * stride) for i in range(n)])  8.01 us
    unnamed x4, local copies, waits for them, and re-layouts  0.91 us
    pallas_call x1, Pallas kernels, local(): pl.pallas_call(functools.partial(last_kernel, children, far), out_shape=j...  0.7 us
  transfers between devices with their start and end apart: 8, of which 3 were waited for; matrix products, arithmetic and copies ran while one was open for 0% of the time, Pallas kernels for 15%

profile of v2, /device:TPU:0, one launch (start us, length us, event | category | flops | bytes accessed | tf_op | source)
XLA Modules:
  0.0 32.5 jit_solution(14227292567953344997)
XLA Ops:
  0.0 4.6 %shard_map.75 = (bf16[528,128]{1,0:T(8,128)(2,1)}, bf16[528,128]{1,0:T(8,128)(2,1)}, bf16[528,128]{1,0:T(8,128)(2,1)}, bf16[528,128]{1,0:T(8,128)(2,1)}) custom-call(s32[2,2048]{1,0:T(2,128)} %refs_0_.3, f32[2,2048]{1,0:T(2,128)} %refs_1_.3, f32[2,2048]{1,0:T(2,128)} %refs_2_.3, s32[2,2048]{1,0:T(2,128)} %refs_3_.3, s32[1,512]{1,0:T(1,128)} %bitcast.2, ...), custom_call_target="tpu_custom_call" | custom-call | flops 1073741824 | bytes 2097152 | tf_op jit(solution)/shard_map/pallas_call | solution.py:159
  4.6 0.0 copy-start.1
  4.6 3.0 %collective-permute-start.4 = (bf16[528,128]{1,0:T(8,128)(2,1)}, bf16[528,128]{1,0:T(8,128)(2,1)S(1)}, u32[]{:S(2)}, u32[]{:S(2)}) collective-permute-start(bf16[528,128]{1,0:T(8,128)(2,1)} %get-tuple-element.27), channel_id=1, source_target_pairs={{0,1},{1,0},{2,3},{3,2},{4,5},{5,4},{6,7},{7,6},{8,9},{9,8},{10,11... | collective-permute-start | bytes 405512 | tf_op jit(solution)/shard_map/ppermute | solution.py:248
  7.6 1.5 %collective-permute-start.5 = (bf16[528,128]{1,0:T(8,128)(2,1)}, bf16[528,128]{1,0:T(8,128)(2,1)S(1)}, u32[]{:S(2)}, u32[]{:S(2)}) collective-permute-start(bf16[528,128]{1,0:T(8,128)(2,1)} %get-tuple-element.28), channel_id=1, source_target_pairs={{0,2},{1,3},{2,0},{3,1},{4,6},{5,7},{6,4},{7,5},{8,10},{9,11},{10,... | collective-permute-start | bytes 405512 | tf_op jit(solution)/shard_map/ppermute | solution.py:248
  9.2 0.0 collective-permute-start.6
  9.2 4.6 %shard_map.73 = (bf16[528,128]{1,0:T(8,128)(2,1)}, bf16[528,128]{1,0:T(8,128)(2,1)}, bf16[528,128]{1,0:T(8,128)(2,1)}, bf16[528,128]{1,0:T(8,128)(2,1)}) custom-call(s32[2,2048]{1,0:T(2,128)} %refs_0_.3, f32[2,2048]{1,0:T(2,128)} %refs_1_.3, f32[2,2048]{1,0:T(2,128)} %refs_2_.3, s32[2,2048]{1,0:T(2,128)} %refs_3_.3, s32[1,512]{1,0:T(1,128)} %bitcast.3, ...), custom_call_target="tpu_custom_call" | custom-call | flops 1073741824 | bytes 2097152 | tf_op jit(solution)/shard_map/pallas_call | solution.py:159
  13.7 2.0 %collective-permute-start = (bf16[528,128]{1,0:T(8,128)(2,1)}, bf16[528,128]{1,0:T(8,128)(2,1)S(1)}, u32[]{:S(2)}, u32[]{:S(2)}) collective-permute-start(bf16[528,128]{1,0:T(8,128)(2,1)} %get-tuple-element.20), channel_id=1, source_target_pairs={{0,1},{1,0},{2,3},{3,2},{4,5},{5,4},{6,7},{7,6},{8,9},{9,8},{10,11... | collective-permute-start | bytes 405512 | tf_op jit(solution)/shard_map/ppermute | solution.py:248
  15.8 1.5 %collective-permute-start.1 = (bf16[528,128]{1,0:T(8,128)(2,1)}, bf16[528,128]{1,0:T(8,128)(2,1)S(1)}, u32[]{:S(2)}, u32[]{:S(2)}) collective-permute-start(bf16[528,128]{1,0:T(8,128)(2,1)} %get-tuple-element.21), channel_id=1, source_target_pairs={{0,2},{1,3},{2,0},{3,1},{4,6},{5,7},{6,4},{7,5},{8,10},{9,11},{10,... | collective-permute-start | bytes 405512 | tf_op jit(solution)/shard_map/ppermute | solution.py:248
  17.3 0.0 collective-permute-done.4.refs_1_
  17.3 0.0 collective-permute-start.2
  17.3 0.0 collective-permute-done.5.refs_2_
  17.3 0.0 collective-permute-done.6.refs_3_
  17.3 0.0 copy-done.1
  17.3 0.1 shard_map.76
  17.4 3.1 %collective-permute-start.7 = (bf16[272,128]{1,0:T(8,128)(2,1)S(1)}, bf16[272,128]{1,0:T(8,128)(2,1)S(1)}, u32[]{:S(2)}, u32[]{:S(2)}) collective-permute-start(bf16[272,128]{1,0:T(8,128)(2,1)S(1)} %get-tuple-element.32), channel_id=1, source_target_pairs={{0,4},{1,5},{2,6},{3,7},{4,0},{5,1},{6,2},{7,3},{8,12},{9,13},{10,... | collective-permute-start | bytes 208904 | tf_op jit(solution)/shard_map/ppermute | solution.py:248
  20.5 0.0 collective-permute-done.refs_1_
  20.5 2.6 %collective-permute-done.1.refs_2_ = bf16[528,128]{1,0:T(8,128)(2,1)S(1)} collective-permute-done((bf16[528,128]{1,0:T(8,128)(2,1)}, bf16[528,128]{1,0:T(8,128)(2,1)S(1)}, u32[]{:S(2)}, u32[]{:S(2)}) %collective-permute-start.1) | collective-permute-done | bytes 135200 | tf_op jit(solution)/shard_map/ppermute | solution.py:248
  23.1 1.8 %collective-permute-done.2.refs_3_ = bf16[528,128]{1,0:T(8,128)(2,1)S(1)} collective-permute-done((bf16[528,128]{1,0:T(8,128)(2,1)}, bf16[528,128]{1,0:T(8,128)(2,1)S(1)}, u32[]{:S(2)}, u32[]{:S(2)}) %collective-permute-start.2) | collective-permute-done | bytes 135200 | tf_op jit(solution)/shard_map/ppermute | solution.py:248
  24.9 0.0 copy-start
  24.9 0.9 %copy-done = bf16[528,128]{1,0:T(8,128)(2,1)S(1)} copy-done((bf16[528,128]{1,0:T(8,128)(2,1)S(1)}, bf16[528,128]{1,0:T(8,128)(2,1)}, u32[]{:S(2)}) %copy-start) | copy-done | bytes 135192
  25.8 0.1 shard_map.74
  25.9 2.3 %collective-permute-start.3 = (bf16[272,128]{1,0:T(8,128)(2,1)S(1)}, bf16[272,128]{1,0:T(8,128)(2,1)S(1)}, u32[]{:S(2)}, u32[]{:S(2)}) collective-permute-start(bf16[272,128]{1,0:T(8,128)(2,1)S(1)} %get-tuple-element.25), channel_id=1, source_target_pairs={{0,4},{1,5},{2,6},{3,7},{4,0},{5,1},{6,2},{7,3},{8,12},{9,13},{10,... | collective-permute-start | bytes 208904 | tf_op jit(solution)/shard_map/ppermute | solution.py:248
  28.2 0.0 collective-permute-done.7.refs_5_
  28.2 3.6 %collective-permute-done.3.refs_2_ = bf16[272,128]{1,0:T(8,128)(2,1)S(1)} collective-permute-done((bf16[272,128]{1,0:T(8,128)(2,1)S(1)}, bf16[272,128]{1,0:T(8,128)(2,1)S(1)}, u32[]{:S(2)}, u32[]{:S(2)}) %collective-permute-start.3) | collective-permute-done | bytes 69664 | tf_op jit(solution)/shard_map/ppermute | solution.py:248
  31.8 0.7 %shard_map.77 = bf16[2,64,512]{2,1,0:T(8,128)(2,1)} custom-call(f32[256,128]{1,0:T(8,128)S(1)} %get-tuple-element.23.refs_0_, f32[4,128]{1,0:T(4,128)S(1)} %get-tuple-element.24.refs_1_, bf16[272,128]{1,0:T(8,128)(2,1)S(1)} %collective-permute-done.3.refs_2_, f32[256,128]{1,0:T(8,128)S(1)} %get-tuple-element.30.refs_3_, ...), custom_call_target="tpu_custom_call" | custom-call | tf_op jit(solution)/shard_map/pallas_call | solution.py:269
Async XLA Ops:
  4.6 12.7 %copy-start.1 = (bf16[528,128]{1,0:T(8,128)(2,1)S(1)}, bf16[528,128]{1,0:T(8,128)(2,1)}, u32[]{:S(2)}) copy-start(bf16[528,128]{1,0:T(8,128)(2,1)} %get-tuple-element.26.refs_0_) | copy-start | bytes 405508
  4.6 12.7 %collective-permute-start.4 = (bf16[528,128]{1,0:T(8,128)(2,1)}, bf16[528,128]{1,0:T(8,128)(2,1)S(1)}, u32[]{:S(2)}, u32[]{:S(2)}) collective-permute-start(bf16[528,128]{1,0:T(8,128)(2,1)} %get-tuple-element.27), channel_id=1, source_target_pairs={{0,1},{1,0},{2,3},{3,2},{4,5},{5,4},{6,7},{7,6},{8,9},{9,8},{10,11... | collective-permute-start | bytes 405512 | tf_op jit(solution)/shard_map/ppermute | solution.py:248
  7.6 9.7 %collective-permute-start.5 = (bf16[528,128]{1,0:T(8,128)(2,1)}, bf16[528,128]{1,0:T(8,128)(2,1)S(1)}, u32[]{:S(2)}, u32[]{:S(2)}) collective-permute-start(bf16[528,128]{1,0:T(8,128)(2,1)} %get-tuple-element.28), channel_id=1, source_target_pairs={{0,2},{1,3},{2,0},{3,1},{4,6},{5,7},{6,4},{7,5},{8,10},{9,11},{10,... | collective-permute-start | bytes 405512 | tf_op jit(solution)/shard_map/ppermute | solution.py:248
  9.2 8.1 %collective-permute-start.6 = (bf16[528,128]{1,0:T(8,128)(2,1)}, bf16[528,128]{1,0:T(8,128)(2,1)S(1)}, u32[]{:S(2)}, u32[]{:S(2)}) collective-permute-start(bf16[528,128]{1,0:T(8,128)(2,1)} %get-tuple-element.29), channel_id=1, source_target_pairs={{0,3},{1,2},{2,1},{3,0},{4,7},{5,6},{6,5},{7,4},{8,11},{9,10},{10,... | collective-permute-start | bytes 405512 | tf_op jit(solution)/shard_map/ppermute | solution.py:248
  13.7 6.7 %collective-permute-start = (bf16[528,128]{1,0:T(8,128)(2,1)}, bf16[528,128]{1,0:T(8,128)(2,1)S(1)}, u32[]{:S(2)}, u32[]{:S(2)}) collective-permute-start(bf16[528,128]{1,0:T(8,128)(2,1)} %get-tuple-element.20), channel_id=1, source_target_pairs={{0,1},{1,0},{2,3},{3,2},{4,5},{5,4},{6,7},{7,6},{8,9},{9,8},{10,11... | collective-permute-start | bytes 405512 | tf_op jit(solution)/shard_map/ppermute | solution.py:248
  15.8 7.4 %collective-permute-start.1 = (bf16[528,128]{1,0:T(8,128)(2,1)}, bf16[528,128]{1,0:T(8,128)(2,1)S(1)}, u32[]{:S(2)}, u32[]{:S(2)}) collective-permute-start(bf16[528,128]{1,0:T(8,128)(2,1)} %get-tuple-element.21), channel_id=1, source_target_pairs={{0,2},{1,3},{2,0},{3,1},{4,6},{5,7},{6,4},{7,5},{8,10},{9,11},{10,... | collective-permute-start | bytes 405512 | tf_op jit(solution)/shard_map/ppermute | solution.py:248
  17.3 7.6 %collective-permute-start.2 = (bf16[528,128]{1,0:T(8,128)(2,1)}, bf16[528,128]{1,0:T(8,128)(2,1)S(1)}, u32[]{:S(2)}, u32[]{:S(2)}) collective-permute-start(bf16[528,128]{1,0:T(8,128)(2,1)} %get-tuple-element.22), channel_id=1, source_target_pairs={{0,3},{1,2},{2,1},{3,0},{4,7},{5,6},{6,5},{7,4},{8,11},{9,10},{10,... | collective-permute-start | bytes 405512 | tf_op jit(solution)/shard_map/ppermute | solution.py:248
  17.4 10.8 %collective-permute-start.7 = (bf16[272,128]{1,0:T(8,128)(2,1)S(1)}, bf16[272,128]{1,0:T(8,128)(2,1)S(1)}, u32[]{:S(2)}, u32[]{:S(2)}) collective-permute-start(bf16[272,128]{1,0:T(8,128)(2,1)S(1)} %get-tuple-element.32), channel_id=1, source_target_pairs={{0,4},{1,5},{2,6},{3,7},{4,0},{5,1},{6,2},{7,3},{8,12},{9,13},{10,... | collective-permute-start | bytes 208904 | tf_op jit(solution)/shard_map/ppermute | solution.py:248
  24.9 0.9 %copy-start = (bf16[528,128]{1,0:T(8,128)(2,1)S(1)}, bf16[528,128]{1,0:T(8,128)(2,1)}, u32[]{:S(2)}) copy-start(bf16[528,128]{1,0:T(8,128)(2,1)} %get-tuple-element.19.refs_0_) | copy-start | bytes 405508
  25.9 5.9 %collective-permute-start.3 = (bf16[272,128]{1,0:T(8,128)(2,1)S(1)}, bf16[272,128]{1,0:T(8,128)(2,1)S(1)}, u32[]{:S(2)}, u32[]{:S(2)}) collective-permute-start(bf16[272,128]{1,0:T(8,128)(2,1)S(1)} %get-tuple-element.25), channel_id=1, source_target_pairs={{0,4},{1,5},{2,6},{3,7},{4,0},{5,1},{6,2},{7,3},{8,12},{9,13},{10,... | collective-permute-start | bytes 208904 | tf_op jit(solution)/shard_map/ppermute | solution.py:248

commit v3 on v0

v3 whole, which is shorter than its diff:
```python
import functools

import jax
import jax.numpy as jnp
from jax import lax
from jax.experimental import pallas as pl
from jax.experimental.pallas import tpu as pltpu
from jax.sharding import PartitionSpec as P

LANES = 128
VMEM = pl.BlockSpec(memory_space=pltpu.VMEM)
ANY = pl.BlockSpec(memory_space=pl.ANY)
F32, BF16 = jnp.float32, jnp.bfloat16
SMALL = pltpu.CompilerParams(vmem_limit_bytes=6 * 2**20)
LARGE = pltpu.CompilerParams(vmem_limit_bytes=24 * 2**20)


def radices(n):
    near = min(4, max(1, n // 2))
    return near, n // near


def tail_rows(tiles):
    return -(-3 * tiles // 16) * 16


def write_tail(total, ref):
    tiles = total.shape[0]
    high = total.astype(BF16).astype(F32)
    rest = total - high
    middle = rest.astype(BF16).astype(F32)
    pieces = [high, middle, rest - middle]
    spare = tail_rows(tiles) - 3 * tiles
    if spare:
        pieces.append(jnp.zeros((spare, LANES), F32))
    ref[ref.shape[0] - tail_rows(tiles) :, :] = jnp.concatenate(pieces, axis=0).astype(BF16)


def read_tail(ref, tiles):
    tail = ref[ref.shape[0] - tail_rows(tiles) :, :].astype(F32)
    return (tail[2 * tiles : 3 * tiles] + tail[tiles : 2 * tiles]) + tail[:tiles]


def multiply(vec, panel, first_tile, near, groups, outs):
    block = vec.shape[0] // (near * groups)
    me = lax.rem(lax.axis_index("col"), near)
    order = [(group, k) for group in range(groups) for k in range(near)]
    left = jnp.concatenate(
        [
            vec[pl.ds(pl.multiple_of((group * near + jnp.bitwise_xor(me, k)) * block, block), block), :]
            for group, k in order
        ],
        axis=0,
    )
    value = lax.dot_general(
        left, panel[...], (((1,), (1,)), ((), ())), preferred_element_type=F32
    ).astype(BF16)
    for place, (group, k) in enumerate(order):
        for tile in range(value.shape[1] // LANES):
            target = ((first_tile + tile) * groups + group) * block
            outs[k][target : target + block, :] = value[
                place * block : (place + 1) * block, tile * LANES : (tile + 1) * LANES
            ]


def away_kernel(near, far, width, *refs):
    pos_ref, frac_ref, weight_ref, kept_ref, root_ref, off_ref, vec_ref = refs[:7]
    outs = refs[7 : 7 + near]
    own_vec, panels, vec, poles, pole_in, kept_in, root_in, index_in, roots, sums, sems, in_sems = refs[7 + near :]
    children, cols, depth = panels.shape
    tiles = cols // LANES
    chunk = own_vec.shape[1]
    me = lax.div(lax.axis_index("col"), near)

    small = [
        pltpu.make_async_copy(source, target, in_sems.at[number])
        for number, (source, target) in enumerate(
            (
                (root_ref, index_in),
                (off_ref, root_in),
                (pos_ref, kept_in.at[0]),
                (frac_ref, pole_in.at[0]),
                (weight_ref, pole_in.at[1]),
                (kept_ref, kept_in.at[1]),
            )
        )
    ]
    large = [
        [
            pltpu.make_async_copy(
                vec_ref.at[child, pl.ds(pl.multiple_of(jnp.bitwise_xor(me, j) * chunk, chunk), chunk), :],
                vec.at[child, pl.ds((j - 1) * chunk, chunk), :] if j else own_vec.at[child],
                sems.at[child, j],
            )
            for j in range(far)
        ]
        for child in range(children)
    ]
    for copy in small:
        copy.start()
    for copies in large:
        for copy in copies[1:]:
            copy.start()
    for copy in small:
        copy.wait()
    for copies in large:
        copies[0].start()

    both = jnp.concatenate([index_in[...].astype(F32), root_in[...], jnp.zeros((6, cols), F32)], axis=0).T
    for number in range(2):
        roots[number] = jnp.broadcast_to(both[:, number : number + 1], (cols, LANES))
    for child in range(children):
        own = slice(child, child + 1)
        poles[child, 0] = jnp.broadcast_to(kept_in[0, own, :].astype(F32), (8, depth))
        poles[child, 1] = jnp.broadcast_to(pole_in[0, own, :], (8, depth))
        scaled = kept_in[1, own, :].astype(F32) * pole_in[1, own, :]
        poles[child, 2] = jnp.broadcast_to(scaled, (8, depth))

    def form(child, first_col):
        for row in range(first_col, first_col + width, 16):
            at = slice(row, row + 16)
            root = roots[0, at, :].reshape(2, 8, LANES)
            off = roots[1, at, :].reshape(2, 8, LANES)
            total = sums[at, :].reshape(2, 8, LANES) if child else jnp.zeros((2, 8, LANES), F32)
            for first in range(0, depth, LANES):
                here = slice(first, first + LANES)
                spacing = (poles[child, 0, :, here] - root) + (poles[child, 1, :, here] - off)
                raw = poles[child, 2, :, here] * pl.reciprocal(spacing, approx=True)
                total = total + raw * raw
                panels[child, at, here] = raw.reshape(16, LANES).astype(BF16)
            sums[at, :] = total.reshape(16, LANES)

    units = [(child, first) for child in range(children) for first in range(0, cols, width)]
    form(*units[0])
    for number, (child, first) in enumerate(units):
        if first == 0:
            for copy in large[child][1:]:
                copy.wait()
        if number + 1 < len(units):
            form(*units[number + 1])
        else:
            total = jnp.concatenate(
                [
                    jnp.sum(sums[at : at + LANES, :].T, axis=0, keepdims=True)
                    for at in range(0, cols, LANES)
                ],
                axis=0,
            )
            for out in outs:
                write_tail(total, out)
        panel = panels.at[child, first : first + width, :]
        multiply(vec.at[child], panel, child * tiles + first // LANES, near, far - 1, outs)
    for copies in large:
        copies[0].wait()


def own_kernel(near, width, vec, panels, *outs):
    children, cols, _ = panels.shape
    for child in range(children):
        for first in range(0, cols, width):
            panel = panels.at[child, first : first + width, :]
            multiply(vec.at[child], panel, (child * cols + first) // LANES, near, 1, outs)


def child_calls(near, far, poles, roots, vectors):
    children, rows, depth = vectors.shape
    cols = roots[0].shape[1]
    width = min(256, cols)
    tiles = cols // LANES
    chunk = rows // far
    block = chunk // near
    flops = 2 * children * chunk * depth * cols
    *away, own_vec, panels = pl.pallas_call(
        functools.partial(away_kernel, near, far, width),
        out_shape=[pltpu.VMEM((children * tiles * (far - 1) * block + tail_rows(tiles), LANES), BF16)] * near
        + [pltpu.VMEM((children, chunk, depth), BF16), pltpu.VMEM((children, cols, depth), BF16)],
        in_specs=[ANY] * 7,
        out_specs=[VMEM] * (near + 2),
        scratch_shapes=[
            pltpu.VMEM((children, rows - chunk, depth), BF16),
            pltpu.VMEM((children, 3, 8, depth), F32),
            pltpu.VMEM((2, children, depth), F32),
            pltpu.VMEM((2, children, depth), jnp.int32),
            pltpu.VMEM((1, cols), F32),
            pltpu.VMEM((1, cols), jnp.int32),
            pltpu.VMEM((2, cols, LANES), F32),
            pltpu.VMEM((cols, LANES), F32),
            pltpu.SemaphoreType.DMA((children, far)),
            pltpu.SemaphoreType.DMA((6,)),
        ],
        compiler_params=LARGE,
        cost_estimate=pl.CostEstimate(
            flops=flops * (far - 1),
            bytes_accessed=2 * children * rows * depth,
            transcendentals=children * depth * cols,
        ),
    )(*(pltpu.with_memory_space_constraint(x, pltpu.HBM) for x in (*poles, *roots, vectors)))
    own = pl.pallas_call(
        functools.partial(own_kernel, near, width),
        out_shape=[pltpu.VMEM((children * tiles * block, LANES), BF16)] * near,
        in_specs=[VMEM] * 2,
        out_specs=[VMEM] * near,
        compiler_params=LARGE,
        cost_estimate=pl.CostEstimate(flops=flops, bytes_accessed=0, transcendentals=0),
    )(own_vec, panels)
    return away, own


def middle_kernel(near, tiles, block, *refs):
    parts, total_ref, outs = refs[:near], refs[near + 1], refs[near + 2 :]
    total = read_tail(parts[0], tiles)
    for part in parts[1:]:
        total = total + read_tail(part, tiles)
    total_ref[...] = total
    groups = len(outs)
    rows = outs[0].shape[0] - tail_rows(tiles)
    size = rows if groups == 1 else block
    for group, out in enumerate(outs):
        write_tail(total, out)
        for first in range(0, rows, size):
            at = slice(first * groups + group * size, first * groups + (group + 1) * size)
            value = parts[0][at, :].astype(F32)
            for part in parts[1:]:
                value = value + part[at, :].astype(F32)
            out[first : first + size, :] = value.astype(BF16)


def middle_call(near, far, tiles, block, parts, after):
    rows = (parts[0].shape[0] - tail_rows(tiles)) // (far - 1)
    return pl.pallas_call(
        functools.partial(middle_kernel, near, tiles, block),
        out_shape=[jax.ShapeDtypeStruct((tiles, LANES), F32)]
        + [jax.ShapeDtypeStruct((rows + tail_rows(tiles), LANES), BF16)] * (far - 1),
        in_specs=[VMEM] * near + [ANY],
        out_specs=[VMEM] * far,
        compiler_params=SMALL,
    )(*parts, after)


def sum_kernel(*refs):
    value = refs[0][...].astype(F32)
    for part in refs[1:-1]:
        value = value + part[...].astype(F32)
    refs[-1][...] = value


def sum_call(parts):
    return pl.pallas_call(
        sum_kernel,
        out_shape=jax.ShapeDtypeStruct(parts[0].shape, F32),
        in_specs=[VMEM] * len(parts),
        out_specs=VMEM,
        compiler_params=SMALL,
        cost_estimate=pl.CostEstimate(flops=4 * 10**10, bytes_accessed=0, transcendentals=0),
    )(*parts)


def last_kernel(*refs):
    total_ref, own, others, out_ref = refs[0], refs[1], refs[2:-1], refs[-1]
    children, block, cols = out_ref.shape
    tiles = cols // LANES
    total = total_ref[...]
    for other in others:
        total = total + read_tail(other, tiles)
    scale = lax.rsqrt(total)
    for child in range(children):
        for tile in range(tiles):
            at = slice((child * tiles + tile) * block, (child * tiles + tile + 1) * block)
            value = own[at, :]
            for part in others:
                value = value + part[at, :].astype(F32)
            out_ref[child, :, tile * LANES : (tile + 1) * LANES] = (
                value * scale[tile : tile + 1, :]
            ).astype(BF16)


def exchange(parts, stride, n):
    got = list(parts)
    for k in sorted(range(1, len(parts)), key=lambda k: (k.bit_count(), -k)):
        got[k] = lax.ppermute(parts[k], "col", [(i, i ^ (k * stride)) for i in range(n)])
    return got


def solution(mesh):
    n = mesh.shape["col"]
    near, far = radices(n)

    def local(vectors, position, fraction, weight, retained, root_index, root_offset):
        children, rows, _ = vectors.shape
        cols = root_index.shape[0]
        block = rows // n
        roots = (root_index[None, :], root_offset[None, :])
        poles = (position, fraction, weight, retained)
        away, own = child_calls(near, far, poles, roots, vectors)
        away = exchange(away, 1, n)
        total, *sums = middle_call(near, far, cols // LANES, block, away, own[0])
        own = sum_call(exchange(own, 1, n))
        others = exchange([total] + sums, near, n)[1:]
        return pl.pallas_call(
            last_kernel,
            out_shape=jax.ShapeDtypeStruct((children, block, cols), BF16),
            in_specs=[VMEM] * (2 + len(others)),
            out_specs=VMEM,
            compiler_params=SMALL,
        )(total, own, *others)

    return jax.shard_map(
        local,
        mesh=mesh,
        in_specs=(P(None, "row", "col"),) + (P(None, "col"),) * 4 + (P(), P()),
        out_specs=P(None, ("row", "col"), None),
        check_vma=False,
    )
```

time: 140 us -> 24.8 us (0.18)
  the two profiles are of different devices: /device:TPU:0 before, /device:TPU:6 now
where the time goes in v3:
time: 24.8 us; the launch traced here: 24.6 us
  starting transfers between devices  9.76 us (39%)
  waiting for transfers between devices  8.5 us (34%)
  Pallas kernels  6.35 us (26%)
    ppermute x7, starting transfers between devices, exchange(): lax.ppermute(parts[k], 'col', [(i, i ^ k * stride) for i in range(n)])  9.76 us
    ppermute x7, waiting for transfers between devices, exchange(): lax.ppermute(parts[k], 'col', [(i, i ^ k * stride) for i in range(n)])  8.5 us
    pallas_call x1, Pallas kernels, child_calls(): pl.pallas_call(functools.partial(away_kernel, near, far, width), out_shap...  4.24 us
    pallas_call x1, Pallas kernels, child_calls(): pl.pallas_call(functools.partial(own_kernel, near, width), out_shape=[plt...  1.28 us
    pallas_call x1, Pallas kernels, local(): pl.pallas_call(last_kernel, out_shape=jax.ShapeDtypeStruct((children, blo...  0.7 us
  transfers between devices with their start and end apart: 7, of which 4 were waited for; matrix products, arithmetic and copies ran while one was open for 0% of the time, Pallas kernels for 6%

profile of v3, /device:TPU:6, one launch (start us, length us, event | category | flops | bytes accessed | tf_op | source)
XLA Modules:
  0.0 24.6 jit_solution(3648500451011312525)
XLA Ops:
  0.0 4.2 %shard_map.73 = (bf16[528,128]{1,0:T(8,128)(2,1)S(1)}, bf16[528,128]{1,0:T(8,128)(2,1)S(1)}, bf16[528,128]{1,0:T(8,128)(2,1)S(1)}, bf16[528,128]{1,0:T(8,128)(2,...) custom-call(s32[2,2048]{1,0:T(2,128)} %refs_0_.1, f32[2,2048]{1,0:T(2,128)} %refs_1_.1, ...), custom_call_target="tpu_custom_call" | custom-call | flops 1073741824 | bytes 4194304 | tf_op jit(solution)/shard_map/pallas_call | solution.py:173
  4.2 0.6 %collective-permute-start = (bf16[528,128]{1,0:T(8,128)(2,1)S(1)}, bf16[528,128]{1,0:T(8,128)(2,1)S(1)}, u32[]{:S(2)}, u32[]{:S(2)}) collective-permute-start(bf16[528,128]{1,0:T(8,128)(2,1)S(1)} %get-tuple-element.18), channel_id=1, source_target_pairs={{0,1},{1,0},{2,3},{3,2},{4,5},{5,4},{6,7},{7,6},{8,9},{9,8},{10,11... | collective-permute-start | bytes 405512 | tf_op jit(solution)/shard_map/ppermute | solution.py:280
  4.8 1.6 %collective-permute-start.1 = (bf16[528,128]{1,0:T(8,128)(2,1)S(1)}, bf16[528,128]{1,0:T(8,128)(2,1)S(1)}, u32[]{:S(2)}, u32[]{:S(2)}) collective-permute-start(bf16[528,128]{1,0:T(8,128)(2,1)S(1)} %get-tuple-element.19), channel_id=1, source_target_pairs={{0,2},{1,3},{2,0},{3,1},{4,6},{5,7},{6,4},{7,5},{8,10},{9,11},{10,... | collective-permute-start | bytes 405512 | tf_op jit(solution)/shard_map/ppermute | solution.py:280
  6.4 1.4 %collective-permute-start.2 = (bf16[528,128]{1,0:T(8,128)(2,1)S(1)}, bf16[528,128]{1,0:T(8,128)(2,1)S(1)}, u32[]{:S(2)}, u32[]{:S(2)}) collective-permute-start(bf16[528,128]{1,0:T(8,128)(2,1)S(1)} %get-tuple-element.20), channel_id=1, source_target_pairs={{0,3},{1,2},{2,1},{3,0},{4,7},{5,6},{6,5},{7,4},{8,11},{9,10},{10,... | collective-permute-start | bytes 405512 | tf_op jit(solution)/shard_map/ppermute | solution.py:280
  7.8 1.3 %shard_map.74 = (bf16[512,128]{1,0:T(8,128)(2,1)S(1)}, bf16[512,128]{1,0:T(8,128)(2,1)S(1)}, bf16[512,128]{1,0:T(8,128)(2,1)S(1)}, bf16[512,128]{1,0:T(8,128)(2,1)S(1)}) custom-call(bf16[2,256,2048]{2,1,0:T(8,128)(2,1)S(1)} %get-tuple-element.21.vec, bf16[2,512,2048]{2,1,0:T(8,128)(2,1)S(1)} %get-tuple-element.22.panels), custom_call_target="tpu_custom_call" | custom-call | flops 1073741824 | tf_op jit(solution)/shard_map/pallas_call | solution.py:198
  9.1 0.6 %collective-permute-start.3 = (bf16[512,128]{1,0:T(8,128)(2,1)S(1)}, bf16[512,128]{1,0:T(8,128)(2,1)S(1)}, u32[]{:S(2)}, u32[]{:S(2)}) collective-permute-start(bf16[512,128]{1,0:T(8,128)(2,1)S(1)} %get-tuple-element.25), channel_id=1, source_target_pairs={{0,1},{1,0},{2,3},{3,2},{4,5},{5,4},{6,7},{7,6},{8,9},{9,8},{10,11... | collective-permute-start | bytes 393224 | tf_op jit(solution)/shard_map/ppermute | solution.py:280
  9.7 1.6 %collective-permute-start.4 = (bf16[512,128]{1,0:T(8,128)(2,1)S(1)}, bf16[512,128]{1,0:T(8,128)(2,1)S(1)}, u32[]{:S(2)}, u32[]{:S(2)}) collective-permute-start(bf16[512,128]{1,0:T(8,128)(2,1)S(1)} %get-tuple-element.26), channel_id=1, source_target_pairs={{0,2},{1,3},{2,0},{3,1},{4,6},{5,7},{6,4},{7,5},{8,10},{9,11},{10,... | collective-permute-start | bytes 393224 | tf_op jit(solution)/shard_map/ppermute | solution.py:280
  11.3 0.0 collective-permute-done.refs_1_
  11.3 1.4 %collective-permute-start.5 = (bf16[512,128]{1,0:T(8,128)(2,1)S(1)}, bf16[512,128]{1,0:T(8,128)(2,1)S(1)}, u32[]{:S(2)}, u32[]{:S(2)}) collective-permute-start(bf16[512,128]{1,0:T(8,128)(2,1)S(1)} %get-tuple-element.27), channel_id=1, source_target_pairs={{0,3},{1,2},{2,1},{3,0},{4,7},{5,6},{6,5},{7,4},{8,11},{9,10},{10,... | collective-permute-start | bytes 393224 | tf_op jit(solution)/shard_map/ppermute | solution.py:280
  12.6 0.0 collective-permute-done.1.refs_2_
  12.7 2.6 %collective-permute-done.2.refs_3_ = bf16[528,128]{1,0:T(8,128)(2,1)S(1)} collective-permute-done((bf16[528,128]{1,0:T(8,128)(2,1)S(1)}, bf16[528,128]{1,0:T(8,128)(2,1)S(1)}, u32[]{:S(2)}, u32[]{:S(2)}) %collective-permute-start.2) | collective-permute-done | bytes 135200 | tf_op jit(solution)/shard_map/ppermute | solution.py:280
  15.2 0.1 shard_map.75
  15.3 2.7 %collective-permute-start.6 = (bf16[528,128]{1,0:T(8,128)(2,1)S(1)}, bf16[528,128]{1,0:T(8,128)(2,1)S(1)}, u32[]{:S(2)}, u32[]{:S(2)}) collective-permute-start(bf16[528,128]{1,0:T(8,128)(2,1)S(1)} %get-tuple-element.28), channel_id=1, source_target_pairs={{0,4},{1,5},{2,6},{3,7},{4,0},{5,1},{6,2},{7,3},{8,12},{9,13},{10,... | collective-permute-start | bytes 405512 | tf_op jit(solution)/shard_map/ppermute | solution.py:280
  17.9 0.0 collective-permute-done.3.refs_1_
  17.9 0.2 collective-permute-done.4.refs_2_
  18.2 4.1 %collective-permute-done.5.refs_3_ = bf16[512,128]{1,0:T(8,128)(2,1)S(1)} collective-permute-done((bf16[512,128]{1,0:T(8,128)(2,1)S(1)}, bf16[512,128]{1,0:T(8,128)(2,1)S(1)}, u32[]{:S(2)}, u32[]{:S(2)}) %collective-permute-start.5) | collective-permute-done | bytes 131104 | tf_op jit(solution)/shard_map/ppermute | solution.py:280
  22.2 0.1 shard_map.76.refs_1_
  22.3 1.6 %collective-permute-done.6.refs_2_ = bf16[528,128]{1,0:T(8,128)(2,1)S(1)} collective-permute-done((bf16[528,128]{1,0:T(8,128)(2,1)S(1)}, bf16[528,128]{1,0:T(8,128)(2,1)S(1)}, u32[]{:S(2)}, u32[]{:S(2)}) %collective-permute-start.6) | collective-permute-done | bytes 135200 | tf_op jit(solution)/shard_map/ppermute | solution.py:280
  23.9 0.7 %shard_map.77 = bf16[2,64,512]{2,1,0:T(8,128)(2,1)} custom-call(f32[4,128]{1,0:T(4,128)S(1)} %get-tuple-element.24.refs_0_, f32[512,128]{1,0:T(8,128)S(1)} %shard_map.76.refs_1_, bf16[528,128]{1,0:T(8,128)(2,1)S(1)} %collective-permute-done.6.refs_2_), custom_call_target="tpu_custom_call" | custom-call | tf_op jit(solution)/shard_map/pallas_call | solution.py:299
Async XLA Ops:
  4.2 7.0 %collective-permute-start = (bf16[528,128]{1,0:T(8,128)(2,1)S(1)}, bf16[528,128]{1,0:T(8,128)(2,1)S(1)}, u32[]{:S(2)}, u32[]{:S(2)}) collective-permute-start(bf16[528,128]{1,0:T(8,128)(2,1)S(1)} %get-tuple-element.18), channel_id=1, source_target_pairs={{0,1},{1,0},{2,3},{3,2},{4,5},{5,4},{6,7},{7,6},{8,9},{9,8},{10,11... | collective-permute-start | bytes 405512 | tf_op jit(solution)/shard_map/ppermute | solution.py:280
  4.8 7.8 %collective-permute-start.1 = (bf16[528,128]{1,0:T(8,128)(2,1)S(1)}, bf16[528,128]{1,0:T(8,128)(2,1)S(1)}, u32[]{:S(2)}, u32[]{:S(2)}) collective-permute-start(bf16[528,128]{1,0:T(8,128)(2,1)S(1)} %get-tuple-element.19), channel_id=1, source_target_pairs={{0,2},{1,3},{2,0},{3,1},{4,6},{5,7},{6,4},{7,5},{8,10},{9,11},{10,... | collective-permute-start | bytes 405512 | tf_op jit(solution)/shard_map/ppermute | solution.py:280
  6.4 8.8 %collective-permute-start.2 = (bf16[528,128]{1,0:T(8,128)(2,1)S(1)}, bf16[528,128]{1,0:T(8,128)(2,1)S(1)}, u32[]{:S(2)}, u32[]{:S(2)}) collective-permute-start(bf16[528,128]{1,0:T(8,128)(2,1)S(1)} %get-tuple-element.20), channel_id=1, source_target_pairs={{0,3},{1,2},{2,1},{3,0},{4,7},{5,6},{6,5},{7,4},{8,11},{9,10},{10,... | collective-permute-start | bytes 405512 | tf_op jit(solution)/shard_map/ppermute | solution.py:280
  9.1 8.8 %collective-permute-start.3 = (bf16[512,128]{1,0:T(8,128)(2,1)S(1)}, bf16[512,128]{1,0:T(8,128)(2,1)S(1)}, u32[]{:S(2)}, u32[]{:S(2)}) collective-permute-start(bf16[512,128]{1,0:T(8,128)(2,1)S(1)} %get-tuple-element.25), channel_id=1, source_target_pairs={{0,1},{1,0},{2,3},{3,2},{4,5},{5,4},{6,7},{7,6},{8,9},{9,8},{10,11... | collective-permute-start | bytes 393224 | tf_op jit(solution)/shard_map/ppermute | solution.py:280
  9.7 8.5 %collective-permute-start.4 = (bf16[512,128]{1,0:T(8,128)(2,1)S(1)}, bf16[512,128]{1,0:T(8,128)(2,1)S(1)}, u32[]{:S(2)}, u32[]{:S(2)}) collective-permute-start(bf16[512,128]{1,0:T(8,128)(2,1)S(1)} %get-tuple-element.26), channel_id=1, source_target_pairs={{0,2},{1,3},{2,0},{3,1},{4,6},{5,7},{6,4},{7,5},{8,10},{9,11},{10,... | collective-permute-start | bytes 393224 | tf_op jit(solution)/shard_map/ppermute | solution.py:280
  11.3 11.0 %collective-permute-start.5 = (bf16[512,128]{1,0:T(8,128)(2,1)S(1)}, bf16[512,128]{1,0:T(8,128)(2,1)S(1)}, u32[]{:S(2)}, u32[]{:S(2)}) collective-permute-start(bf16[512,128]{1,0:T(8,128)(2,1)S(1)} %get-tuple-element.27), channel_id=1, source_target_pairs={{0,3},{1,2},{2,1},{3,0},{4,7},{5,6},{6,5},{7,4},{8,11},{9,10},{10,... | collective-permute-start | bytes 393224 | tf_op jit(solution)/shard_map/ppermute | solution.py:280
  15.3 8.7 %collective-permute-start.6 = (bf16[528,128]{1,0:T(8,128)(2,1)S(1)}, bf16[528,128]{1,0:T(8,128)(2,1)S(1)}, u32[]{:S(2)}, u32[]{:S(2)}) collective-permute-start(bf16[528,128]{1,0:T(8,128)(2,1)S(1)} %get-tuple-element.28), channel_id=1, source_target_pairs={{0,4},{1,5},{2,6},{3,7},{4,0},{5,1},{6,2},{7,3},{8,12},{9,13},{10,... | collective-permute-start | bytes 405512 | tf_op jit(solution)/shard_map/ppermute | solution.py:280

commit v4 on v3

--- a/solution.py
+++ b/solution.py
@@ -92,18 +92,18 @@
                 vec.at[child, pl.ds((j - 1) * chunk, chunk), :] if j else own_vec.at[child],
                 sems.at[child, j],
             )
-            for j in range(far)
+            for j in range(1 if child + 1 == children else 0, far)
         ]
         for child in range(children)
     ]
     for copy in small:
         copy.start()
     for copies in large:
-        for copy in copies[1:]:
+        for copy in copies[1 - far :]:
             copy.start()
     for copy in small:
         copy.wait()
-    for copies in large:
+    for copies in large[:-1]:
         copies[0].start()
 
     both = jnp.concatenate([index_in[...].astype(F32), root_in[...], jnp.zeros((6, cols), F32)], axis=0).T
@@ -134,7 +134,7 @@
     form(*units[0])
     for number, (child, first) in enumerate(units):
         if first == 0:
-            for copy in large[child][1:]:
+            for copy in large[child][1 - far :]:
                 copy.wait()
         if number + 1 < len(units):
             form(*units[number + 1])
@@ -150,16 +150,25 @@
                 write_tail(total, out)
         panel = panels.at[child, first : first + width, :]
         multiply(vec.at[child], panel, child * tiles + first // LANES, near, far - 1, outs)
-    for copies in large:
+    for copies in large[:-1]:
         copies[0].wait()
 
 
-def own_kernel(near, width, vec, panels, *outs):
+def own_kernel(near, width, own_vec, panels, vec_ref, *refs):
+    outs, (last_vec, sem) = refs[:near], refs[near:]
     children, cols, _ = panels.shape
+    chunk = last_vec.shape[0]
+    me = lax.div(lax.axis_index("col"), near)
+    rows = pl.ds(pl.multiple_of(me * chunk, chunk), chunk)
+    copy = pltpu.make_async_copy(vec_ref.at[children - 1, rows, :], last_vec, sem)
+    copy.start()
     for child in range(children):
+        vec = last_vec if child + 1 == children else own_vec.at[child]
+        if child + 1 == children:
+            copy.wait()
         for first in range(0, cols, width):
             panel = panels.at[child, first : first + width, :]
-            multiply(vec.at[child], panel, (child * cols + first) // LANES, near, 1, outs)
+            multiply(vec, panel, (child * cols + first) // LANES, near, 1, outs)
 
 
 def child_calls(near, far, poles, roots, vectors):
@@ -170,10 +179,11 @@
     chunk = rows // far
     block = chunk // near
     flops = 2 * children * chunk * depth * cols
+    vectors = pltpu.with_memory_space_constraint(vectors, pltpu.HBM)
     *away, own_vec, panels = pl.pallas_call(
         functools.partial(away_kernel, near, far, width),
         out_shape=[pltpu.VMEM((children * tiles * (far - 1) * block + tail_rows(tiles), LANES), BF16)] * near
-        + [pltpu.VMEM((children, chunk, depth), BF16), pltpu.VMEM((children, cols, depth), BF16)],
+        + [pltpu.VMEM((children - 1, chunk, depth), BF16), pltpu.VMEM((children, cols, depth), BF16)],
         in_specs=[ANY] * 7,
         out_specs=[VMEM] * (near + 2),
         scratch_shapes=[
@@ -194,15 +204,16 @@
             bytes_accessed=2 * children * rows * depth,
             transcendentals=children * depth * cols,
         ),
-    )(*(pltpu.with_memory_space_constraint(x, pltpu.HBM) for x in (*poles, *roots, vectors)))
+    )(*(pltpu.with_memory_space_constraint(x, pltpu.HBM) for x in (*poles, *roots)), vectors)
     own = pl.pallas_call(
         functools.partial(own_kernel, near, width),
         out_shape=[pltpu.VMEM((children * tiles * block, LANES), BF16)] * near,
-        in_specs=[VMEM] * 2,
+        in_specs=[VMEM, VMEM, ANY],
         out_specs=[VMEM] * near,
+        scratch_shapes=[pltpu.VMEM((chunk, depth), BF16), pltpu.SemaphoreType.DMA],
         compiler_params=LARGE,
         cost_estimate=pl.CostEstimate(flops=flops, bytes_accessed=0, transcendentals=0),
-    )(own_vec, panels)
+    )(own_vec, panels, vectors)
     return away, own
 
 

time: 24.8 us -> 24.5 us (0.988)
  the two profiles are of different devices: /device:TPU:6 before, /device:TPU:0 now
where the time goes in v4:
time: 24.5 us; the launch traced here: 24.3 us
  starting transfers between devices  11 us (45%)
  Pallas kernels  7.6 us (31%)
  waiting for transfers between devices  5.7 us (23%)
    ppermute x7, starting transfers between devices, exchange(): lax.ppermute(parts[k], 'col', [(i, i ^ k * stride) for i in range(n)])  11 us
    ppermute x7, waiting for transfers between devices, exchange(): lax.ppermute(parts[k], 'col', [(i, i ^ k * stride) for i in range(n)])  5.7 us
    pallas_call x1, Pallas kernels, child_calls(): pl.pallas_call(functools.partial(away_kernel, near, far, width), out_shap...  4.24 us
    pallas_call x1, Pallas kernels, child_calls(): pl.pallas_call(functools.partial(own_kernel, near, width), out_shape=[plt...  2.53 us
    pallas_call x1, Pallas kernels, local(): pl.pallas_call(last_kernel, out_shape=jax.ShapeDtypeStruct((children, blo...  0.7 us
  transfers between devices with their start and end apart: 7, of which 4 were waited for; matrix products, arithmetic and copies ran while one was open for 0% of the time, Pallas kernels for 11%

profile of v4, /device:TPU:0, one launch (start us, length us, event | category | flops | bytes accessed | tf_op | source)
XLA Modules:
  0.0 24.3 jit_solution(8841528111487473324)
XLA Ops:
  0.0 4.2 %shard_map.73 = (bf16[528,128]{1,0:T(8,128)(2,1)S(1)}, bf16[528,128]{1,0:T(8,128)(2,1)S(1)}, bf16[528,128]{1,0:T(8,128)(2,1)S(1)}, bf16[528,128]{1,0:T(8,128)(2,...) custom-call(s32[2,2048]{1,0:T(2,128)} %refs_0_.1, f32[2,2048]{1,0:T(2,128)} %refs_1_.1, ...), custom_call_target="tpu_custom_call" | custom-call | flops 1073741824 | bytes 4194304 | tf_op jit(solution)/shard_map/pallas_call | solution.py:183
  4.2 3.0 %collective-permute-start = (bf16[528,128]{1,0:T(8,128)(2,1)S(1)}, bf16[528,128]{1,0:T(8,128)(2,1)S(1)}, u32[]{:S(2)}, u32[]{:S(2)}) collective-permute-start(bf16[528,128]{1,0:T(8,128)(2,1)S(1)} %get-tuple-element.18), channel_id=1, source_target_pairs={{0,1},{1,0},{2,3},{3,2},{4,5},{5,4},{6,7},{7,6},{8,9},{9,8},{10,11... | collective-permute-start | bytes 405512 | tf_op jit(solution)/shard_map/ppermute | solution.py:291
  7.3 1.6 %collective-permute-start.1 = (bf16[528,128]{1,0:T(8,128)(2,1)S(1)}, bf16[528,128]{1,0:T(8,128)(2,1)S(1)}, u32[]{:S(2)}, u32[]{:S(2)}) collective-permute-start(bf16[528,128]{1,0:T(8,128)(2,1)S(1)} %get-tuple-element.19), channel_id=1, source_target_pairs={{0,2},{1,3},{2,0},{3,1},{4,6},{5,7},{6,4},{7,5},{8,10},{9,11},{10,... | collective-permute-start | bytes 405512 | tf_op jit(solution)/shard_map/ppermute | solution.py:291
  8.8 0.0 collective-permute-start.2
  8.8 2.5 %shard_map.74 = (bf16[512,128]{1,0:T(8,128)(2,1)S(1)}, bf16[512,128]{1,0:T(8,128)(2,1)S(1)}, bf16[512,128]{1,0:T(8,128)(2,1)S(1)}, bf16[512,128]{1,0:T(8,128)(2,1)S(1)}) custom-call(bf16[1,256,2048]{2,1,0:T(8,128)(2,1)S(1)} %get-tuple-element.21.own_vec, bf16[2,512,2048]{2,1,0:T(8,128)(2,1)S(1)} %get-tuple-element.22.panels, bf16[2,512,2048]{2,1,0:T(8,128)(2,1)} %vec_ref.1), custom_call_target="tpu_custom_call" | custom-call | flops 1073741824 | tf_op jit(solution)/shard_map/pallas_call | solution.py:208
  11.4 2.0 %collective-permute-start.3 = (bf16[512,128]{1,0:T(8,128)(2,1)S(1)}, bf16[512,128]{1,0:T(8,128)(2,1)S(1)}, u32[]{:S(2)}, u32[]{:S(2)}) collective-permute-start(bf16[512,128]{1,0:T(8,128)(2,1)S(1)} %get-tuple-element.25), channel_id=1, source_target_pairs={{0,1},{1,0},{2,3},{3,2},{4,5},{5,4},{6,7},{7,6},{8,9},{9,8},{10,11... | collective-permute-start | bytes 393224 | tf_op jit(solution)/shard_map/ppermute | solution.py:291
  13.3 1.6 %collective-permute-start.4 = (bf16[512,128]{1,0:T(8,128)(2,1)S(1)}, bf16[512,128]{1,0:T(8,128)(2,1)S(1)}, u32[]{:S(2)}, u32[]{:S(2)}) collective-permute-start(bf16[512,128]{1,0:T(8,128)(2,1)S(1)} %get-tuple-element.26), channel_id=1, source_target_pairs={{0,2},{1,3},{2,0},{3,1},{4,6},{5,7},{6,4},{7,5},{8,10},{9,11},{10,... | collective-permute-start | bytes 393224 | tf_op jit(solution)/shard_map/ppermute | solution.py:291
  14.9 0.0 collective-permute-done.refs_1_
  14.9 0.0 collective-permute-start.5
  14.9 0.0 collective-permute-done.1.refs_2_
  14.9 0.5 %collective-permute-done.2.refs_3_ = bf16[528,128]{1,0:T(8,128)(2,1)S(1)} collective-permute-done((bf16[528,128]{1,0:T(8,128)(2,1)S(1)}, bf16[528,128]{1,0:T(8,128)(2,1)S(1)}, u32[]{:S(2)}, u32[]{:S(2)}) %collective-permute-start.2) | collective-permute-done | bytes 135200 | tf_op jit(solution)/shard_map/ppermute | solution.py:291
  15.5 0.1 shard_map.75
  15.6 2.8 %collective-permute-start.6 = (bf16[528,128]{1,0:T(8,128)(2,1)S(1)}, bf16[528,128]{1,0:T(8,128)(2,1)S(1)}, u32[]{:S(2)}, u32[]{:S(2)}) collective-permute-start(bf16[528,128]{1,0:T(8,128)(2,1)S(1)} %get-tuple-element.28), channel_id=1, source_target_pairs={{0,4},{1,5},{2,6},{3,7},{4,0},{5,1},{6,2},{7,3},{8,12},{9,13},{10,... | collective-permute-start | bytes 405512 | tf_op jit(solution)/shard_map/ppermute | solution.py:291
  18.4 0.1 collective-permute-done.3.refs_1_
  18.5 3.8 %collective-permute-done.4.refs_2_ = bf16[512,128]{1,0:T(8,128)(2,1)S(1)} collective-permute-done((bf16[512,128]{1,0:T(8,128)(2,1)S(1)}, bf16[512,128]{1,0:T(8,128)(2,1)S(1)}, u32[]{:S(2)}, u32[]{:S(2)}) %collective-permute-start.4) | collective-permute-done | bytes 131104 | tf_op jit(solution)/shard_map/ppermute | solution.py:291
  22.3 1.2 %collective-permute-done.5.refs_3_ = bf16[512,128]{1,0:T(8,128)(2,1)S(1)} collective-permute-done((bf16[512,128]{1,0:T(8,128)(2,1)S(1)}, bf16[512,128]{1,0:T(8,128)(2,1)S(1)}, u32[]{:S(2)}, u32[]{:S(2)}) %collective-permute-start.5) | collective-permute-done | bytes 131104 | tf_op jit(solution)/shard_map/ppermute | solution.py:291
  23.5 0.1 shard_map.76.refs_1_
  23.6 0.0 collective-permute-done.6.refs_2_
  23.6 0.7 %shard_map.77 = bf16[2,64,512]{2,1,0:T(8,128)(2,1)} custom-call(f32[4,128]{1,0:T(4,128)S(1)} %get-tuple-element.24.refs_0_, f32[512,128]{1,0:T(8,128)S(1)} %shard_map.76.refs_1_, bf16[528,128]{1,0:T(8,128)(2,1)S(1)} %collective-permute-done.6.refs_2_), custom_call_target="tpu_custom_call" | custom-call | tf_op jit(solution)/shard_map/pallas_call | solution.py:310
Async XLA Ops:
  4.2 10.7 %collective-permute-start = (bf16[528,128]{1,0:T(8,128)(2,1)S(1)}, bf16[528,128]{1,0:T(8,128)(2,1)S(1)}, u32[]{:S(2)}, u32[]{:S(2)}) collective-permute-start(bf16[528,128]{1,0:T(8,128)(2,1)S(1)} %get-tuple-element.18), channel_id=1, source_target_pairs={{0,1},{1,0},{2,3},{3,2},{4,5},{5,4},{6,7},{7,6},{8,9},{9,8},{10,11... | collective-permute-start | bytes 405512 | tf_op jit(solution)/shard_map/ppermute | solution.py:291
  7.3 7.7 %collective-permute-start.1 = (bf16[528,128]{1,0:T(8,128)(2,1)S(1)}, bf16[528,128]{1,0:T(8,128)(2,1)S(1)}, u32[]{:S(2)}, u32[]{:S(2)}) collective-permute-start(bf16[528,128]{1,0:T(8,128)(2,1)S(1)} %get-tuple-element.19), channel_id=1, source_target_pairs={{0,2},{1,3},{2,0},{3,1},{4,6},{5,7},{6,4},{7,5},{8,10},{9,11},{10,... | collective-permute-start | bytes 405512 | tf_op jit(solution)/shard_map/ppermute | solution.py:291
  8.8 6.6 %collective-permute-start.2 = (bf16[528,128]{1,0:T(8,128)(2,1)S(1)}, bf16[528,128]{1,0:T(8,128)(2,1)S(1)}, u32[]{:S(2)}, u32[]{:S(2)}) collective-permute-start(bf16[528,128]{1,0:T(8,128)(2,1)S(1)} %get-tuple-element.20), channel_id=1, source_target_pairs={{0,3},{1,2},{2,1},{3,0},{4,7},{5,6},{6,5},{7,4},{8,11},{9,10},{10,... | collective-permute-start | bytes 405512 | tf_op jit(solution)/shard_map/ppermute | solution.py:291
  11.4 7.1 %collective-permute-start.3 = (bf16[512,128]{1,0:T(8,128)(2,1)S(1)}, bf16[512,128]{1,0:T(8,128)(2,1)S(1)}, u32[]{:S(2)}, u32[]{:S(2)}) collective-permute-start(bf16[512,128]{1,0:T(8,128)(2,1)S(1)} %get-tuple-element.25), channel_id=1, source_target_pairs={{0,1},{1,0},{2,3},{3,2},{4,5},{5,4},{6,7},{7,6},{8,9},{9,8},{10,11... | collective-permute-start | bytes 393224 | tf_op jit(solution)/shard_map/ppermute | solution.py:291
  13.3 9.0 %collective-permute-start.4 = (bf16[512,128]{1,0:T(8,128)(2,1)S(1)}, bf16[512,128]{1,0:T(8,128)(2,1)S(1)}, u32[]{:S(2)}, u32[]{:S(2)}) collective-permute-start(bf16[512,128]{1,0:T(8,128)(2,1)S(1)} %get-tuple-element.26), channel_id=1, source_target_pairs={{0,2},{1,3},{2,0},{3,1},{4,6},{5,7},{6,4},{7,5},{8,10},{9,11},{10,... | collective-permute-start | bytes 393224 | tf_op jit(solution)/shard_map/ppermute | solution.py:291
  14.9 8.6 %collective-permute-start.5 = (bf16[512,128]{1,0:T(8,128)(2,1)S(1)}, bf16[512,128]{1,0:T(8,128)(2,1)S(1)}, u32[]{:S(2)}, u32[]{:S(2)}) collective-permute-start(bf16[512,128]{1,0:T(8,128)(2,1)S(1)} %get-tuple-element.27), channel_id=1, source_target_pairs={{0,3},{1,2},{2,1},{3,0},{4,7},{5,6},{6,5},{7,4},{8,11},{9,10},{10,... | collective-permute-start | bytes 393224 | tf_op jit(solution)/shard_map/ppermute | solution.py:291
  15.6 8.1 %collective-permute-start.6 = (bf16[528,128]{1,0:T(8,128)(2,1)S(1)}, bf16[528,128]{1,0:T(8,128)(2,1)S(1)}, u32[]{:S(2)}, u32[]{:S(2)}) collective-permute-start(bf16[528,128]{1,0:T(8,128)(2,1)S(1)} %get-tuple-element.28), channel_id=1, source_target_pairs={{0,4},{1,5},{2,6},{3,7},{4,0},{5,1},{6,2},{7,3},{8,12},{9,13},{10,... | collective-permute-start | bytes 405512 | tf_op jit(solution)/shard_map/ppermute | solution.py:291

commit v5 on v4

--- a/solution.py
+++ b/solution.py
@@ -101,22 +101,28 @@
     for copies in large:
         for copy in copies[1 - far :]:
             copy.start()
-    for copy in small:
+    for copy in small[:2]:
+        copy.wait()
+    both = jnp.concatenate([index_in[...].astype(F32), root_in[...], jnp.zeros((6, cols), F32)], axis=0).T
+    for copy in small[2:]:
         copy.wait()
     for copies in large[:-1]:
         copies[0].start()
 
-    both = jnp.concatenate([index_in[...].astype(F32), root_in[...], jnp.zeros((6, cols), F32)], axis=0).T
-    for number in range(2):
-        roots[number] = jnp.broadcast_to(both[:, number : number + 1], (cols, LANES))
-    for child in range(children):
-        own = slice(child, child + 1)
-        poles[child, 0] = jnp.broadcast_to(kept_in[0, own, :].astype(F32), (8, depth))
-        poles[child, 1] = jnp.broadcast_to(pole_in[0, own, :], (8, depth))
-        scaled = kept_in[1, own, :].astype(F32) * pole_in[1, own, :]
-        poles[child, 2] = jnp.broadcast_to(scaled, (8, depth))
+    def prepare(child, first_col):
+        if child == 0:
+            here = slice(first_col, first_col + width)
+            for number in range(2):
+                roots[number, here, :] = jnp.broadcast_to(both[here, number : number + 1], (width, LANES))
+        if first_col == 0:
+            own = slice(child, child + 1)
+            poles[child, 0] = jnp.broadcast_to(kept_in[0, own, :].astype(F32), (8, depth))
+            poles[child, 1] = jnp.broadcast_to(pole_in[0, own, :], (8, depth))
+            scaled = kept_in[1, own, :].astype(F32) * pole_in[1, own, :]
+            poles[child, 2] = jnp.broadcast_to(scaled, (8, depth))
 
     def form(child, first_col):
+        prepare(child, first_col)
         for row in range(first_col, first_col + width, 16):
             at = slice(row, row + 16)
             root = roots[0, at, :].reshape(2, 8, LANES)

time: 24.5 us -> 24.4 us (level)
  no operation moved by 1% of the time
where the time goes in v5:
time: 24.4 us; the launch traced here: 24.2 us
  starting transfers between devices  11 us (45%)
  Pallas kernels  7.51 us (31%)
  waiting for transfers between devices  5.72 us (23%)
    ppermute x7, starting transfers between devices, exchange(): lax.ppermute(parts[k], 'col', [(i, i ^ k * stride) for i in range(n)])  11 us
    ppermute x7, waiting for transfers between devices, exchange(): lax.ppermute(parts[k], 'col', [(i, i ^ k * stride) for i in range(n)])  5.72 us
    pallas_call x1, Pallas kernels, child_calls(): pl.pallas_call(functools.partial(away_kernel, near, far, width), out_shap...  4.15 us
    pallas_call x1, Pallas kernels, child_calls(): pl.pallas_call(functools.partial(own_kernel, near, width), out_shape=[plt...  2.53 us
    pallas_call x1, Pallas kernels, local(): pl.pallas_call(last_kernel, out_shape=jax.ShapeDtypeStruct((children, blo...  0.7 us
  transfers between devices with their start and end apart: 7, of which 4 were waited for; matrix products, arithmetic and copies ran while one was open for 0% of the time, Pallas kernels for 11%

profile of v5, /device:TPU:0, one launch (start us, length us, event | category | flops | bytes accessed | tf_op | source)
XLA Modules:
  0.0 24.2 jit_solution(550055126436789109)
XLA Ops:
  0.0 4.2 %shard_map.73 = (bf16[528,128]{1,0:T(8,128)(2,1)S(1)}, bf16[528,128]{1,0:T(8,128)(2,1)S(1)}, bf16[528,128]{1,0:T(8,128)(2,1)S(1)}, bf16[528,128]{1,0:T(8,128)(2,...) custom-call(s32[2,2048]{1,0:T(2,128)} %refs_0_.1, f32[2,2048]{1,0:T(2,128)} %refs_1_.1, ...), custom_call_target="tpu_custom_call" | custom-call | flops 1073741824 | bytes 4194304 | tf_op jit(solution)/shard_map/pallas_call | solution.py:189
  4.2 3.0 %collective-permute-start = (bf16[528,128]{1,0:T(8,128)(2,1)S(1)}, bf16[528,128]{1,0:T(8,128)(2,1)S(1)}, u32[]{:S(2)}, u32[]{:S(2)}) collective-permute-start(bf16[528,128]{1,0:T(8,128)(2,1)S(1)} %get-tuple-element.18), channel_id=1, source_target_pairs={{0,1},{1,0},{2,3},{3,2},{4,5},{5,4},{6,7},{7,6},{8,9},{9,8},{10,11... | collective-permute-start | bytes 405512 | tf_op jit(solution)/shard_map/ppermute | solution.py:297
  7.2 1.6 %collective-permute-start.1 = (bf16[528,128]{1,0:T(8,128)(2,1)S(1)}, bf16[528,128]{1,0:T(8,128)(2,1)S(1)}, u32[]{:S(2)}, u32[]{:S(2)}) collective-permute-start(bf16[528,128]{1,0:T(8,128)(2,1)S(1)} %get-tuple-element.19), channel_id=1, source_target_pairs={{0,2},{1,3},{2,0},{3,1},{4,6},{5,7},{6,4},{7,5},{8,10},{9,11},{10,... | collective-permute-start | bytes 405512 | tf_op jit(solution)/shard_map/ppermute | solution.py:297
  8.7 0.0 collective-permute-start.2
  8.7 2.5 %shard_map.74 = (bf16[512,128]{1,0:T(8,128)(2,1)S(1)}, bf16[512,128]{1,0:T(8,128)(2,1)S(1)}, bf16[512,128]{1,0:T(8,128)(2,1)S(1)}, bf16[512,128]{1,0:T(8,128)(2,1)S(1)}) custom-call(bf16[1,256,2048]{2,1,0:T(8,128)(2,1)S(1)} %get-tuple-element.21.own_vec, bf16[2,512,2048]{2,1,0:T(8,128)(2,1)S(1)} %get-tuple-element.22.panels, bf16[2,512,2048]{2,1,0:T(8,128)(2,1)} %vec_ref.1), custom_call_target="tpu_custom_call" | custom-call | flops 1073741824 | tf_op jit(solution)/shard_map/pallas_call | solution.py:214
  11.3 2.0 %collective-permute-start.3 = (bf16[512,128]{1,0:T(8,128)(2,1)S(1)}, bf16[512,128]{1,0:T(8,128)(2,1)S(1)}, u32[]{:S(2)}, u32[]{:S(2)}) collective-permute-start(bf16[512,128]{1,0:T(8,128)(2,1)S(1)} %get-tuple-element.25), channel_id=1, source_target_pairs={{0,1},{1,0},{2,3},{3,2},{4,5},{5,4},{6,7},{7,6},{8,9},{9,8},{10,11... | collective-permute-start | bytes 393224 | tf_op jit(solution)/shard_map/ppermute | solution.py:297
  13.3 1.6 %collective-permute-start.4 = (bf16[512,128]{1,0:T(8,128)(2,1)S(1)}, bf16[512,128]{1,0:T(8,128)(2,1)S(1)}, u32[]{:S(2)}, u32[]{:S(2)}) collective-permute-start(bf16[512,128]{1,0:T(8,128)(2,1)S(1)} %get-tuple-element.26), channel_id=1, source_target_pairs={{0,2},{1,3},{2,0},{3,1},{4,6},{5,7},{6,4},{7,5},{8,10},{9,11},{10,... | collective-permute-start | bytes 393224 | tf_op jit(solution)/shard_map/ppermute | solution.py:297
  14.8 0.0 collective-permute-done.refs_1_
  14.8 0.0 collective-permute-start.5
  14.8 0.0 collective-permute-done.1.refs_2_
  14.8 0.6 %collective-permute-done.2.refs_3_ = bf16[528,128]{1,0:T(8,128)(2,1)S(1)} collective-permute-done((bf16[528,128]{1,0:T(8,128)(2,1)S(1)}, bf16[528,128]{1,0:T(8,128)(2,1)S(1)}, u32[]{:S(2)}, u32[]{:S(2)}) %collective-permute-start.2) | collective-permute-done | bytes 135200 | tf_op jit(solution)/shard_map/ppermute | solution.py:297
  15.4 0.1 shard_map.75
  15.5 2.8 %collective-permute-start.6 = (bf16[528,128]{1,0:T(8,128)(2,1)S(1)}, bf16[528,128]{1,0:T(8,128)(2,1)S(1)}, u32[]{:S(2)}, u32[]{:S(2)}) collective-permute-start(bf16[528,128]{1,0:T(8,128)(2,1)S(1)} %get-tuple-element.28), channel_id=1, source_target_pairs={{0,4},{1,5},{2,6},{3,7},{4,0},{5,1},{6,2},{7,3},{8,12},{9,13},{10,... | collective-permute-start | bytes 405512 | tf_op jit(solution)/shard_map/ppermute | solution.py:297
  18.3 0.1 collective-permute-done.3.refs_1_
  18.4 3.8 %collective-permute-done.4.refs_2_ = bf16[512,128]{1,0:T(8,128)(2,1)S(1)} collective-permute-done((bf16[512,128]{1,0:T(8,128)(2,1)S(1)}, bf16[512,128]{1,0:T(8,128)(2,1)S(1)}, u32[]{:S(2)}, u32[]{:S(2)}) %collective-permute-start.4) | collective-permute-done | bytes 131104 | tf_op jit(solution)/shard_map/ppermute | solution.py:297
  22.2 1.2 %collective-permute-done.5.refs_3_ = bf16[512,128]{1,0:T(8,128)(2,1)S(1)} collective-permute-done((bf16[512,128]{1,0:T(8,128)(2,1)S(1)}, bf16[512,128]{1,0:T(8,128)(2,1)S(1)}, u32[]{:S(2)}, u32[]{:S(2)}) %collective-permute-start.5) | collective-permute-done | bytes 131104 | tf_op jit(solution)/shard_map/ppermute | solution.py:297
  23.5 0.1 shard_map.76.refs_1_
  23.5 0.0 collective-permute-done.6.refs_2_
  23.5 0.7 %shard_map.77 = bf16[2,64,512]{2,1,0:T(8,128)(2,1)} custom-call(f32[4,128]{1,0:T(4,128)S(1)} %get-tuple-element.24.refs_0_, f32[512,128]{1,0:T(8,128)S(1)} %shard_map.76.refs_1_, bf16[528,128]{1,0:T(8,128)(2,1)S(1)} %collective-permute-done.6.refs_2_), custom_call_target="tpu_custom_call" | custom-call | tf_op jit(solution)/shard_map/pallas_call | solution.py:316
Async XLA Ops:
  4.2 10.7 %collective-permute-start = (bf16[528,128]{1,0:T(8,128)(2,1)S(1)}, bf16[528,128]{1,0:T(8,128)(2,1)S(1)}, u32[]{:S(2)}, u32[]{:S(2)}) collective-permute-start(bf16[528,128]{1,0:T(8,128)(2,1)S(1)} %get-tuple-element.18), channel_id=1, source_target_pairs={{0,1},{1,0},{2,3},{3,2},{4,5},{5,4},{6,7},{7,6},{8,9},{9,8},{10,11... | collective-permute-start | bytes 405512 | tf_op jit(solution)/shard_map/ppermute | solution.py:297
  7.2 7.7 %collective-permute-start.1 = (bf16[528,128]{1,0:T(8,128)(2,1)S(1)}, bf16[528,128]{1,0:T(8,128)(2,1)S(1)}, u32[]{:S(2)}, u32[]{:S(2)}) collective-permute-start(bf16[528,128]{1,0:T(8,128)(2,1)S(1)} %get-tuple-element.19), channel_id=1, source_target_pairs={{0,2},{1,3},{2,0},{3,1},{4,6},{5,7},{6,4},{7,5},{8,10},{9,11},{10,... | collective-permute-start | bytes 405512 | tf_op jit(solution)/shard_map/ppermute | solution.py:297
  8.7 6.7 %collective-permute-start.2 = (bf16[528,128]{1,0:T(8,128)(2,1)S(1)}, bf16[528,128]{1,0:T(8,128)(2,1)S(1)}, u32[]{:S(2)}, u32[]{:S(2)}) collective-permute-start(bf16[528,128]{1,0:T(8,128)(2,1)S(1)} %get-tuple-element.20), channel_id=1, source_target_pairs={{0,3},{1,2},{2,1},{3,0},{4,7},{5,6},{6,5},{7,4},{8,11},{9,10},{10,... | collective-permute-start | bytes 405512 | tf_op jit(solution)/shard_map/ppermute | solution.py:297
  11.3 7.1 %collective-permute-start.3 = (bf16[512,128]{1,0:T(8,128)(2,1)S(1)}, bf16[512,128]{1,0:T(8,128)(2,1)S(1)}, u32[]{:S(2)}, u32[]{:S(2)}) collective-permute-start(bf16[512,128]{1,0:T(8,128)(2,1)S(1)} %get-tuple-element.25), channel_id=1, source_target_pairs={{0,1},{1,0},{2,3},{3,2},{4,5},{5,4},{6,7},{7,6},{8,9},{9,8},{10,11... | collective-permute-start | bytes 393224 | tf_op jit(solution)/shard_map/ppermute | solution.py:297
  13.3 9.0 %collective-permute-start.4 = (bf16[512,128]{1,0:T(8,128)(2,1)S(1)}, bf16[512,128]{1,0:T(8,128)(2,1)S(1)}, u32[]{:S(2)}, u32[]{:S(2)}) collective-permute-start(bf16[512,128]{1,0:T(8,128)(2,1)S(1)} %get-tuple-element.26), channel_id=1, source_target_pairs={{0,2},{1,3},{2,0},{3,1},{4,6},{5,7},{6,4},{7,5},{8,10},{9,11},{10,... | collective-permute-start | bytes 393224 | tf_op jit(solution)/shard_map/ppermute | solution.py:297
  14.8 8.6 %collective-permute-start.5 = (bf16[512,128]{1,0:T(8,128)(2,1)S(1)}, bf16[512,128]{1,0:T(8,128)(2,1)S(1)}, u32[]{:S(2)}, u32[]{:S(2)}) collective-permute-start(bf16[512,128]{1,0:T(8,128)(2,1)S(1)} %get-tuple-element.27), channel_id=1, source_target_pairs={{0,3},{1,2},{2,1},{3,0},{4,7},{5,6},{6,5},{7,4},{8,11},{9,10},{10,... | collective-permute-start | bytes 393224 | tf_op jit(solution)/shard_map/ppermute | solution.py:297
  15.5 8.1 %collective-permute-start.6 = (bf16[528,128]{1,0:T(8,128)(2,1)S(1)}, bf16[528,128]{1,0:T(8,128)(2,1)S(1)}, u32[]{:S(2)}, u32[]{:S(2)}) collective-permute-start(bf16[528,128]{1,0:T(8,128)(2,1)S(1)} %get-tuple-element.28), channel_id=1, source_target_pairs={{0,4},{1,5},{2,6},{3,7},{4,0},{5,1},{6,2},{7,3},{8,12},{9,13},{10,... | collective-permute-start | bytes 405512 | tf_op jit(solution)/shard_map/ppermute | solution.py:297

commit v6 on v5

--- a/solution.py
+++ b/solution.py
@@ -165,13 +165,22 @@
     children, cols, _ = panels.shape
     chunk = last_vec.shape[0]
     me = lax.div(lax.axis_index("col"), near)
-    rows = pl.ds(pl.multiple_of(me * chunk, chunk), chunk)
-    copy = pltpu.make_async_copy(vec_ref.at[children - 1, rows, :], last_vec, sem)
-    copy.start()
+    half = chunk // 2
+    copies = [
+        pltpu.make_async_copy(
+            vec_ref.at[children - 1, pl.ds(pl.multiple_of(me * chunk + first, half), half), :],
+            last_vec.at[first : first + half, :],
+            sem.at[first // half],
+        )
+        for first in (0, half)
+    ]
+    for copy in copies:
+        copy.start()
     for child in range(children):
         vec = last_vec if child + 1 == children else own_vec.at[child]
         if child + 1 == children:
-            copy.wait()
+            for copy in copies:
+                copy.wait()
         for first in range(0, cols, width):
             panel = panels.at[child, first : first + width, :]
             multiply(vec, panel, (child * cols + first) // LANES, near, 1, outs)
@@ -216,7 +225,7 @@
         out_shape=[pltpu.VMEM((children * tiles * block, LANES), BF16)] * near,
         in_specs=[VMEM, VMEM, ANY],
         out_specs=[VMEM] * near,
-        scratch_shapes=[pltpu.VMEM((chunk, depth), BF16), pltpu.SemaphoreType.DMA],
+        scratch_shapes=[pltpu.VMEM((chunk, depth), BF16), pltpu.SemaphoreType.DMA((2,))],
         compiler_params=LARGE,
         cost_estimate=pl.CostEstimate(flops=flops, bytes_accessed=0, transcendentals=0),
     )(own_vec, panels, vectors)

time: 24.4 us -> 24.3 us (level)
  no operation moved by 1% of the time
where the time goes in v6:
time: 24.3 us; the launch traced here: 24.2 us
  starting transfers between devices  11 us (45%)
  Pallas kernels  7.5 us (31%)
  waiting for transfers between devices  5.66 us (23%)
    ppermute x7, starting transfers between devices, exchange(): lax.ppermute(parts[k], 'col', [(i, i ^ k * stride) for i in range(n)])  11 us
    ppermute x7, waiting for transfers between devices, exchange(): lax.ppermute(parts[k], 'col', [(i, i ^ k * stride) for i in range(n)])  5.66 us
    pallas_call x1, Pallas kernels, child_calls(): pl.pallas_call(functools.partial(away_kernel, near, far, width), out_shap...  4.15 us
    pallas_call x1, Pallas kernels, child_calls(): pl.pallas_call(functools.partial(own_kernel, near, width), out_shape=[plt...  2.52 us
    pallas_call x1, Pallas kernels, local(): pl.pallas_call(last_kernel, out_shape=jax.ShapeDtypeStruct((children, blo...  0.7 us
  transfers between devices with their start and end apart: 7, of which 4 were waited for; matrix products, arithmetic and copies ran while one was open for 0% of the time, Pallas kernels for 11%

profile of v6, /device:TPU:0, one launch (start us, length us, event | category | flops | bytes accessed | tf_op | source)
XLA Modules:
  0.0 24.2 jit_solution(4198977070394570957)
XLA Ops:
  0.0 4.2 %shard_map.73 = (bf16[528,128]{1,0:T(8,128)(2,1)S(1)}, bf16[528,128]{1,0:T(8,128)(2,1)S(1)}, bf16[528,128]{1,0:T(8,128)(2,1)S(1)}, bf16[528,128]{1,0:T(8,128)(2,...) custom-call(s32[2,2048]{1,0:T(2,128)} %refs_0_.1, f32[2,2048]{1,0:T(2,128)} %refs_1_.1, ...), custom_call_target="tpu_custom_call" | custom-call | flops 1073741824 | bytes 4194304 | tf_op jit(solution)/shard_map/pallas_call | solution.py:198
  4.2 3.0 %collective-permute-start = (bf16[528,128]{1,0:T(8,128)(2,1)S(1)}, bf16[528,128]{1,0:T(8,128)(2,1)S(1)}, u32[]{:S(2)}, u32[]{:S(2)}) collective-permute-start(bf16[528,128]{1,0:T(8,128)(2,1)S(1)} %get-tuple-element.18), channel_id=1, source_target_pairs={{0,1},{1,0},{2,3},{3,2},{4,5},{5,4},{6,7},{7,6},{8,9},{9,8},{10,11... | collective-permute-start | bytes 405512 | tf_op jit(solution)/shard_map/ppermute | solution.py:306
  7.2 1.6 %collective-permute-start.1 = (bf16[528,128]{1,0:T(8,128)(2,1)S(1)}, bf16[528,128]{1,0:T(8,128)(2,1)S(1)}, u32[]{:S(2)}, u32[]{:S(2)}) collective-permute-start(bf16[528,128]{1,0:T(8,128)(2,1)S(1)} %get-tuple-element.19), channel_id=1, source_target_pairs={{0,2},{1,3},{2,0},{3,1},{4,6},{5,7},{6,4},{7,5},{8,10},{9,11},{10,... | collective-permute-start | bytes 405512 | tf_op jit(solution)/shard_map/ppermute | solution.py:306
  8.7 0.0 collective-permute-start.2
  8.7 2.5 %shard_map.74 = (bf16[512,128]{1,0:T(8,128)(2,1)S(1)}, bf16[512,128]{1,0:T(8,128)(2,1)S(1)}, bf16[512,128]{1,0:T(8,128)(2,1)S(1)}, bf16[512,128]{1,0:T(8,128)(2,1)S(1)}) custom-call(bf16[1,256,2048]{2,1,0:T(8,128)(2,1)S(1)} %get-tuple-element.21.own_vec, bf16[2,512,2048]{2,1,0:T(8,128)(2,1)S(1)} %get-tuple-element.22.panels, bf16[2,512,2048]{2,1,0:T(8,128)(2,1)} %vec_ref.1), custom_call_target="tpu_custom_call" | custom-call | flops 1073741824 | tf_op jit(solution)/shard_map/pallas_call | solution.py:223
  11.3 2.0 %collective-permute-start.3 = (bf16[512,128]{1,0:T(8,128)(2,1)S(1)}, bf16[512,128]{1,0:T(8,128)(2,1)S(1)}, u32[]{:S(2)}, u32[]{:S(2)}) collective-permute-start(bf16[512,128]{1,0:T(8,128)(2,1)S(1)} %get-tuple-element.25), channel_id=1, source_target_pairs={{0,1},{1,0},{2,3},{3,2},{4,5},{5,4},{6,7},{7,6},{8,9},{9,8},{10,11... | collective-permute-start | bytes 393224 | tf_op jit(solution)/shard_map/ppermute | solution.py:306
  13.2 1.6 %collective-permute-start.4 = (bf16[512,128]{1,0:T(8,128)(2,1)S(1)}, bf16[512,128]{1,0:T(8,128)(2,1)S(1)}, u32[]{:S(2)}, u32[]{:S(2)}) collective-permute-start(bf16[512,128]{1,0:T(8,128)(2,1)S(1)} %get-tuple-element.26), channel_id=1, source_target_pairs={{0,2},{1,3},{2,0},{3,1},{4,6},{5,7},{6,4},{7,5},{8,10},{9,11},{10,... | collective-permute-start | bytes 393224 | tf_op jit(solution)/shard_map/ppermute | solution.py:306
  14.8 0.0 collective-permute-done.refs_1_
  14.8 0.0 collective-permute-start.5
  14.8 0.0 collective-permute-done.1.refs_2_
  14.8 0.6 %collective-permute-done.2.refs_3_ = bf16[528,128]{1,0:T(8,128)(2,1)S(1)} collective-permute-done((bf16[528,128]{1,0:T(8,128)(2,1)S(1)}, bf16[528,128]{1,0:T(8,128)(2,1)S(1)}, u32[]{:S(2)}, u32[]{:S(2)}) %collective-permute-start.2) | collective-permute-done | bytes 135200 | tf_op jit(solution)/shard_map/ppermute | solution.py:306
  15.4 0.1 shard_map.75
  15.5 2.8 %collective-permute-start.6 = (bf16[528,128]{1,0:T(8,128)(2,1)S(1)}, bf16[528,128]{1,0:T(8,128)(2,1)S(1)}, u32[]{:S(2)}, u32[]{:S(2)}) collective-permute-start(bf16[528,128]{1,0:T(8,128)(2,1)S(1)} %get-tuple-element.28), channel_id=1, source_target_pairs={{0,4},{1,5},{2,6},{3,7},{4,0},{5,1},{6,2},{7,3},{8,12},{9,13},{10,... | collective-permute-start | bytes 405512 | tf_op jit(solution)/shard_map/ppermute | solution.py:306
  18.3 0.1 collective-permute-done.3.refs_1_
  18.4 3.8 %collective-permute-done.4.refs_2_ = bf16[512,128]{1,0:T(8,128)(2,1)S(1)} collective-permute-done((bf16[512,128]{1,0:T(8,128)(2,1)S(1)}, bf16[512,128]{1,0:T(8,128)(2,1)S(1)}, u32[]{:S(2)}, u32[]{:S(2)}) %collective-permute-start.4) | collective-permute-done | bytes 131104 | tf_op jit(solution)/shard_map/ppermute | solution.py:306
  22.2 1.2 %collective-permute-done.5.refs_3_ = bf16[512,128]{1,0:T(8,128)(2,1)S(1)} collective-permute-done((bf16[512,128]{1,0:T(8,128)(2,1)S(1)}, bf16[512,128]{1,0:T(8,128)(2,1)S(1)}, u32[]{:S(2)}, u32[]{:S(2)}) %collective-permute-start.5) | collective-permute-done | bytes 131104 | tf_op jit(solution)/shard_map/ppermute | solution.py:306
  23.4 0.1 shard_map.76.refs_1_
  23.5 0.0 collective-permute-done.6.refs_2_
  23.5 0.7 %shard_map.77 = bf16[2,64,512]{2,1,0:T(8,128)(2,1)} custom-call(f32[4,128]{1,0:T(4,128)S(1)} %get-tuple-element.24.refs_0_, f32[512,128]{1,0:T(8,128)S(1)} %shard_map.76.refs_1_, bf16[528,128]{1,0:T(8,128)(2,1)S(1)} %collective-permute-done.6.refs_2_), custom_call_target="tpu_custom_call" | custom-call | tf_op jit(solution)/shard_map/pallas_call | solution.py:325
Async XLA Ops:
  4.2 10.7 %collective-permute-start = (bf16[528,128]{1,0:T(8,128)(2,1)S(1)}, bf16[528,128]{1,0:T(8,128)(2,1)S(1)}, u32[]{:S(2)}, u32[]{:S(2)}) collective-permute-start(bf16[528,128]{1,0:T(8,128)(2,1)S(1)} %get-tuple-element.18), channel_id=1, source_target_pairs={{0,1},{1,0},{2,3},{3,2},{4,5},{5,4},{6,7},{7,6},{8,9},{9,8},{10,11... | collective-permute-start | bytes 405512 | tf_op jit(solution)/shard_map/ppermute | solution.py:306
  7.2 7.7 %collective-permute-start.1 = (bf16[528,128]{1,0:T(8,128)(2,1)S(1)}, bf16[528,128]{1,0:T(8,128)(2,1)S(1)}, u32[]{:S(2)}, u32[]{:S(2)}) collective-permute-start(bf16[528,128]{1,0:T(8,128)(2,1)S(1)} %get-tuple-element.19), channel_id=1, source_target_pairs={{0,2},{1,3},{2,0},{3,1},{4,6},{5,7},{6,4},{7,5},{8,10},{9,11},{10,... | collective-permute-start | bytes 405512 | tf_op jit(solution)/shard_map/ppermute | solution.py:306
  8.7 6.7 %collective-permute-start.2 = (bf16[528,128]{1,0:T(8,128)(2,1)S(1)}, bf16[528,128]{1,0:T(8,128)(2,1)S(1)}, u32[]{:S(2)}, u32[]{:S(2)}) collective-permute-start(bf16[528,128]{1,0:T(8,128)(2,1)S(1)} %get-tuple-element.20), channel_id=1, source_target_pairs={{0,3},{1,2},{2,1},{3,0},{4,7},{5,6},{6,5},{7,4},{8,11},{9,10},{10,... | collective-permute-start | bytes 405512 | tf_op jit(solution)/shard_map/ppermute | solution.py:306
  11.3 7.2 %collective-permute-start.3 = (bf16[512,128]{1,0:T(8,128)(2,1)S(1)}, bf16[512,128]{1,0:T(8,128)(2,1)S(1)}, u32[]{:S(2)}, u32[]{:S(2)}) collective-permute-start(bf16[512,128]{1,0:T(8,128)(2,1)S(1)} %get-tuple-element.25), channel_id=1, source_target_pairs={{0,1},{1,0},{2,3},{3,2},{4,5},{5,4},{6,7},{7,6},{8,9},{9,8},{10,11... | collective-permute-start | bytes 393224 | tf_op jit(solution)/shard_map/ppermute | solution.py:306
  13.2 9.0 %collective-permute-start.4 = (bf16[512,128]{1,0:T(8,128)(2,1)S(1)}, bf16[512,128]{1,0:T(8,128)(2,1)S(1)}, u32[]{:S(2)}, u32[]{:S(2)}) collective-permute-start(bf16[512,128]{1,0:T(8,128)(2,1)S(1)} %get-tuple-element.26), channel_id=1, source_target_pairs={{0,2},{1,3},{2,0},{3,1},{4,6},{5,7},{6,4},{7,5},{8,10},{9,11},{10,... | collective-permute-start | bytes 393224 | tf_op jit(solution)/shard_map/ppermute | solution.py:306
  14.8 8.6 %collective-permute-start.5 = (bf16[512,128]{1,0:T(8,128)(2,1)S(1)}, bf16[512,128]{1,0:T(8,128)(2,1)S(1)}, u32[]{:S(2)}, u32[]{:S(2)}) collective-permute-start(bf16[512,128]{1,0:T(8,128)(2,1)S(1)} %get-tuple-element.27), channel_id=1, source_target_pairs={{0,3},{1,2},{2,1},{3,0},{4,7},{5,6},{6,5},{7,4},{8,11},{9,10},{10,... | collective-permute-start | bytes 393224 | tf_op jit(solution)/shard_map/ppermute | solution.py:306
  15.5 8.0 %collective-permute-start.6 = (bf16[528,128]{1,0:T(8,128)(2,1)S(1)}, bf16[528,128]{1,0:T(8,128)(2,1)S(1)}, u32[]{:S(2)}, u32[]{:S(2)}) collective-permute-start(bf16[528,128]{1,0:T(8,128)(2,1)S(1)} %get-tuple-element.28), channel_id=1, source_target_pairs={{0,4},{1,5},{2,6},{3,7},{4,0},{5,1},{6,2},{7,3},{8,12},{9,13},{10,... | collective-permute-start | bytes 405512 | tf_op jit(solution)/shard_map/ppermute | solution.py:306

commit v7 on v5

--- a/solution.py
+++ b/solution.py
@@ -273,8 +273,9 @@
 
 
 def last_kernel(*refs):
-    total_ref, own, others, out_ref = refs[0], refs[1], refs[2:-1], refs[-1]
-    children, block, cols = out_ref.shape
+    total_ref, own, others, (out_ref, held, sems) = refs[0], refs[1], refs[2:-3], refs[-3:]
+    children, block, cols = held.shape
+    copies = [pltpu.make_async_copy(held.at[child], out_ref.at[child], sems.at[child]) for child in range(children)]
     tiles = cols // LANES
     total = total_ref[...]
     for other in others:
@@ -286,9 +287,12 @@
             value = own[at, :]
             for part in others:
                 value = value + part[at, :].astype(F32)
-            out_ref[child, :, tile * LANES : (tile + 1) * LANES] = (
+            held[child, :, tile * LANES : (tile + 1) * LANES] = (
                 value * scale[tile : tile + 1, :]
             ).astype(BF16)
+        copies[child].start()
+    for copy in copies:
+        copy.wait()
 
 
 def exchange(parts, stride, n):
@@ -317,7 +321,8 @@
             last_kernel,
             out_shape=jax.ShapeDtypeStruct((children, block, cols), BF16),
             in_specs=[VMEM] * (2 + len(others)),
-            out_specs=VMEM,
+            out_specs=ANY,
+            scratch_shapes=[pltpu.VMEM((children, block, cols), BF16), pltpu.SemaphoreType.DMA((children,))],
             compiler_params=SMALL,
         )(total, own, *others)
 

time: 24.4 us -> 24.4 us (level)
  no operation moved by 1% of the time
where the time goes in v7:
time: 24.4 us; the launch traced here: 24.2 us
  starting transfers between devices  11 us (45%)
  Pallas kernels  7.51 us (31%)
  waiting for transfers between devices  5.72 us (23%)
    ppermute x7, starting transfers between devices, exchange(): lax.ppermute(parts[k], 'col', [(i, i ^ k * stride) for i in range(n)])  11 us
    ppermute x7, waiting for transfers between devices, exchange(): lax.ppermute(parts[k], 'col', [(i, i ^ k * stride) for i in range(n)])  5.72 us
    pallas_call x1, Pallas kernels, child_calls(): pl.pallas_call(functools.partial(away_kernel, near, far, width), out_shap...  4.15 us
    pallas_call x1, Pallas kernels, child_calls(): pl.pallas_call(functools.partial(own_kernel, near, width), out_shape=[plt...  2.53 us
    pallas_call x1, Pallas kernels, local(): pl.pallas_call(last_kernel, out_shape=jax.ShapeDtypeStruct((children, blo...  0.69 us
  transfers between devices with their start and end apart: 7, of which 4 were waited for; matrix products, arithmetic and copies ran while one was open for 0% of the time, Pallas kernels for 11%

profile of v7, /device:TPU:0, one launch (start us, length us, event | category | flops | bytes accessed | tf_op | source)
XLA Modules:
  0.0 24.2 jit_solution(8224406389038305321)
XLA Ops:
  0.0 4.2 %shard_map.73 = (bf16[528,128]{1,0:T(8,128)(2,1)S(1)}, bf16[528,128]{1,0:T(8,128)(2,1)S(1)}, bf16[528,128]{1,0:T(8,128)(2,1)S(1)}, bf16[528,128]{1,0:T(8,128)(2,...) custom-call(s32[2,2048]{1,0:T(2,128)} %refs_0_.1, f32[2,2048]{1,0:T(2,128)} %refs_1_.1, ...), custom_call_target="tpu_custom_call" | custom-call | flops 1073741824 | bytes 4194304 | tf_op jit(solution)/shard_map/pallas_call | solution.py:189
  4.2 3.0 %collective-permute-start = (bf16[528,128]{1,0:T(8,128)(2,1)S(1)}, bf16[528,128]{1,0:T(8,128)(2,1)S(1)}, u32[]{:S(2)}, u32[]{:S(2)}) collective-permute-start(bf16[528,128]{1,0:T(8,128)(2,1)S(1)} %get-tuple-element.18), channel_id=1, source_target_pairs={{0,1},{1,0},{2,3},{3,2},{4,5},{5,4},{6,7},{7,6},{8,9},{9,8},{10,11... | collective-permute-start | bytes 405512 | tf_op jit(solution)/shard_map/ppermute | solution.py:301
  7.2 1.6 %collective-permute-start.1 = (bf16[528,128]{1,0:T(8,128)(2,1)S(1)}, bf16[528,128]{1,0:T(8,128)(2,1)S(1)}, u32[]{:S(2)}, u32[]{:S(2)}) collective-permute-start(bf16[528,128]{1,0:T(8,128)(2,1)S(1)} %get-tuple-element.19), channel_id=1, source_target_pairs={{0,2},{1,3},{2,0},{3,1},{4,6},{5,7},{6,4},{7,5},{8,10},{9,11},{10,... | collective-permute-start | bytes 405512 | tf_op jit(solution)/shard_map/ppermute | solution.py:301
  8.7 0.0 collective-permute-start.2
  8.7 2.5 %shard_map.74 = (bf16[512,128]{1,0:T(8,128)(2,1)S(1)}, bf16[512,128]{1,0:T(8,128)(2,1)S(1)}, bf16[512,128]{1,0:T(8,128)(2,1)S(1)}, bf16[512,128]{1,0:T(8,128)(2,1)S(1)}) custom-call(bf16[1,256,2048]{2,1,0:T(8,128)(2,1)S(1)} %get-tuple-element.21.own_vec, bf16[2,512,2048]{2,1,0:T(8,128)(2,1)S(1)} %get-tuple-element.22.panels, bf16[2,512,2048]{2,1,0:T(8,128)(2,1)} %vec_ref.1), custom_call_target="tpu_custom_call" | custom-call | flops 1073741824 | tf_op jit(solution)/shard_map/pallas_call | solution.py:214
  11.3 2.0 %collective-permute-start.3 = (bf16[512,128]{1,0:T(8,128)(2,1)S(1)}, bf16[512,128]{1,0:T(8,128)(2,1)S(1)}, u32[]{:S(2)}, u32[]{:S(2)}) collective-permute-start(bf16[512,128]{1,0:T(8,128)(2,1)S(1)} %get-tuple-element.25), channel_id=1, source_target_pairs={{0,1},{1,0},{2,3},{3,2},{4,5},{5,4},{6,7},{7,6},{8,9},{9,8},{10,11... | collective-permute-start | bytes 393224 | tf_op jit(solution)/shard_map/ppermute | solution.py:301
  13.3 1.6 %collective-permute-start.4 = (bf16[512,128]{1,0:T(8,128)(2,1)S(1)}, bf16[512,128]{1,0:T(8,128)(2,1)S(1)}, u32[]{:S(2)}, u32[]{:S(2)}) collective-permute-start(bf16[512,128]{1,0:T(8,128)(2,1)S(1)} %get-tuple-element.26), channel_id=1, source_target_pairs={{0,2},{1,3},{2,0},{3,1},{4,6},{5,7},{6,4},{7,5},{8,10},{9,11},{10,... | collective-permute-start | bytes 393224 | tf_op jit(solution)/shard_map/ppermute | solution.py:301
  14.8 0.0 collective-permute-done.refs_1_
  14.8 0.0 collective-permute-start.5
  14.8 0.0 collective-permute-done.1.refs_2_
  14.8 0.6 %collective-permute-done.2.refs_3_ = bf16[528,128]{1,0:T(8,128)(2,1)S(1)} collective-permute-done((bf16[528,128]{1,0:T(8,128)(2,1)S(1)}, bf16[528,128]{1,0:T(8,128)(2,1)S(1)}, u32[]{:S(2)}, u32[]{:S(2)}) %collective-permute-start.2) | collective-permute-done | bytes 135200 | tf_op jit(solution)/shard_map/ppermute | solution.py:301
  15.4 0.1 shard_map.75
  15.5 2.8 %collective-permute-start.6 = (bf16[528,128]{1,0:T(8,128)(2,1)S(1)}, bf16[528,128]{1,0:T(8,128)(2,1)S(1)}, u32[]{:S(2)}, u32[]{:S(2)}) collective-permute-start(bf16[528,128]{1,0:T(8,128)(2,1)S(1)} %get-tuple-element.28), channel_id=1, source_target_pairs={{0,4},{1,5},{2,6},{3,7},{4,0},{5,1},{6,2},{7,3},{8,12},{9,13},{10,... | collective-permute-start | bytes 405512 | tf_op jit(solution)/shard_map/ppermute | solution.py:301
  18.3 0.1 collective-permute-done.3.refs_1_
  18.4 3.8 %collective-permute-done.4.refs_2_ = bf16[512,128]{1,0:T(8,128)(2,1)S(1)} collective-permute-done((bf16[512,128]{1,0:T(8,128)(2,1)S(1)}, bf16[512,128]{1,0:T(8,128)(2,1)S(1)}, u32[]{:S(2)}, u32[]{:S(2)}) %collective-permute-start.4) | collective-permute-done | bytes 131104 | tf_op jit(solution)/shard_map/ppermute | solution.py:301
  22.2 1.2 %collective-permute-done.5.refs_3_ = bf16[512,128]{1,0:T(8,128)(2,1)S(1)} collective-permute-done((bf16[512,128]{1,0:T(8,128)(2,1)S(1)}, bf16[512,128]{1,0:T(8,128)(2,1)S(1)}, u32[]{:S(2)}, u32[]{:S(2)}) %collective-permute-start.5) | collective-permute-done | bytes 131104 | tf_op jit(solution)/shard_map/ppermute | solution.py:301
  23.5 0.1 shard_map.76.refs_1_
  23.5 0.0 collective-permute-done.6.refs_2_
  23.5 0.7 %shard_map.77 = bf16[2,64,512]{2,1,0:T(8,128)(2,1)} custom-call(f32[4,128]{1,0:T(4,128)S(1)} %get-tuple-element.24.refs_0_, f32[512,128]{1,0:T(8,128)S(1)} %shard_map.76.refs_1_, bf16[528,128]{1,0:T(8,128)(2,1)S(1)} %collective-permute-done.6.refs_2_), custom_call_target="tpu_custom_call" | custom-call | tf_op jit(solution)/shard_map/pallas_call | solution.py:320
Async XLA Ops:
  4.2 10.7 %collective-permute-start = (bf16[528,128]{1,0:T(8,128)(2,1)S(1)}, bf16[528,128]{1,0:T(8,128)(2,1)S(1)}, u32[]{:S(2)}, u32[]{:S(2)}) collective-permute-start(bf16[528,128]{1,0:T(8,128)(2,1)S(1)} %get-tuple-element.18), channel_id=1, source_target_pairs={{0,1},{1,0},{2,3},{3,2},{4,5},{5,4},{6,7},{7,6},{8,9},{9,8},{10,11... | collective-permute-start | bytes 405512 | tf_op jit(solution)/shard_map/ppermute | solution.py:301
  7.2 7.7 %collective-permute-start.1 = (bf16[528,128]{1,0:T(8,128)(2,1)S(1)}, bf16[528,128]{1,0:T(8,128)(2,1)S(1)}, u32[]{:S(2)}, u32[]{:S(2)}) collective-permute-start(bf16[528,128]{1,0:T(8,128)(2,1)S(1)} %get-tuple-element.19), channel_id=1, source_target_pairs={{0,2},{1,3},{2,0},{3,1},{4,6},{5,7},{6,4},{7,5},{8,10},{9,11},{10,... | collective-permute-start | bytes 405512 | tf_op jit(solution)/shard_map/ppermute | solution.py:301
  8.7 6.7 %collective-permute-start.2 = (bf16[528,128]{1,0:T(8,128)(2,1)S(1)}, bf16[528,128]{1,0:T(8,128)(2,1)S(1)}, u32[]{:S(2)}, u32[]{:S(2)}) collective-permute-start(bf16[528,128]{1,0:T(8,128)(2,1)S(1)} %get-tuple-element.20), channel_id=1, source_target_pairs={{0,3},{1,2},{2,1},{3,0},{4,7},{5,6},{6,5},{7,4},{8,11},{9,10},{10,... | collective-permute-start | bytes 405512 | tf_op jit(solution)/shard_map/ppermute | solution.py:301
  11.3 7.1 %collective-permute-start.3 = (bf16[512,128]{1,0:T(8,128)(2,1)S(1)}, bf16[512,128]{1,0:T(8,128)(2,1)S(1)}, u32[]{:S(2)}, u32[]{:S(2)}) collective-permute-start(bf16[512,128]{1,0:T(8,128)(2,1)S(1)} %get-tuple-element.25), channel_id=1, source_target_pairs={{0,1},{1,0},{2,3},{3,2},{4,5},{5,4},{6,7},{7,6},{8,9},{9,8},{10,11... | collective-permute-start | bytes 393224 | tf_op jit(solution)/shard_map/ppermute | solution.py:301
  13.3 9.0 %collective-permute-start.4 = (bf16[512,128]{1,0:T(8,128)(2,1)S(1)}, bf16[512,128]{1,0:T(8,128)(2,1)S(1)}, u32[]{:S(2)}, u32[]{:S(2)}) collective-permute-start(bf16[512,128]{1,0:T(8,128)(2,1)S(1)} %get-tuple-element.26), channel_id=1, source_target_pairs={{0,2},{1,3},{2,0},{3,1},{4,6},{5,7},{6,4},{7,5},{8,10},{9,11},{10,... | collective-permute-start | bytes 393224 | tf_op jit(solution)/shard_map/ppermute | solution.py:301
  14.8 8.6 %collective-permute-start.5 = (bf16[512,128]{1,0:T(8,128)(2,1)S(1)}, bf16[512,128]{1,0:T(8,128)(2,1)S(1)}, u32[]{:S(2)}, u32[]{:S(2)}) collective-permute-start(bf16[512,128]{1,0:T(8,128)(2,1)S(1)} %get-tuple-element.27), channel_id=1, source_target_pairs={{0,3},{1,2},{2,1},{3,0},{4,7},{5,6},{6,5},{7,4},{8,11},{9,10},{10,... | collective-permute-start | bytes 393224 | tf_op jit(solution)/shard_map/ppermute | solution.py:301
  15.5 8.1 %collective-permute-start.6 = (bf16[528,128]{1,0:T(8,128)(2,1)S(1)}, bf16[528,128]{1,0:T(8,128)(2,1)S(1)}, u32[]{:S(2)}, u32[]{:S(2)}) collective-permute-start(bf16[528,128]{1,0:T(8,128)(2,1)S(1)} %get-tuple-element.28), channel_id=1, source_target_pairs={{0,4},{1,5},{2,6},{3,7},{4,0},{5,1},{6,2},{7,3},{8,12},{9,13},{10,... | collective-permute-start | bytes 405512 | tf_op jit(solution)/shard_map/ppermute | solution.py:301
